TPU v7x, 32 devices: a whole 2x2x4 slice. The times are simulated.
32 devices in a mesh: dp: 8 (over y, x, core), tensor: 4 (over z).
Axes of the slice: x: 2, y: 2, z: 4, core: 2. Of those that a mesh axis runs over, the one named last changes fastest.
Arguments:
- tokens: bfloat16 [16, 512, 768], P('dp', 'tensor'), may hold values from -6 to 6
- time_embed: float32 [16, 768], P('dp'), may hold values from -6 to 6
- class_embed: float32 [16, 768], P('dp'), may hold values from -6 to 6
- valid_mask: int32 [16, 512], P('dp'), may hold values from 0 to 1, as said below
- routes: int32 [16, 512, 2], P('dp'), may hold values from 0 to 7, all different within a row; in each aligned block of 512 rows (0 to 511, 512 to 1023, ..., all dimensions but the last counted through in order) at most 192 rows name the same one
- gate_logits: float32 [16, 512, 2], P('dp'), may hold values from -4 to 4
- ada_weight: bfloat16 [768, 6, 768], P(None, None, 'tensor'), may hold values from -0.21875 to 0.21875
- ada_bias: bfloat16 [6, 768], replicated, may hold values from -3 to 3
- qkv_weight: bfloat16 [768, 3, 768], P(None, None, 'tensor'), may hold values from -0.21875 to 0.21875
- out_weight: bfloat16 [768, 768], P(None, 'tensor'), may hold values from -0.875 to 0.875
- out_bias: bfloat16 [768], replicated, may hold values from -3 to 3
- fc1_weight: bfloat16 [768, 3072], P(None, 'tensor'), may hold values from -0.21875 to 0.21875
- fc1_bias: bfloat16 [3072], P('tensor'), may hold values from -3 to 3
- fc2_weight: bfloat16 [768, 3072], P(None, 'tensor'), may hold values from -0.109375 to 0.109375
- fc2_bias: bfloat16 [768], replicated, may hold values from -3 to 3
- expert_in: bfloat16 [768, 8, 3072], P(None, None, 'tensor'), may hold values from -0.21875 to 0.21875
- expert_out: bfloat16 [768, 8, 3072], P(None, None, 'tensor'), may hold values from -0.109375 to 0.109375
- out_grad: bfloat16 [16, 512, 768], P('dp', 'tensor'), may hold values from -6 to 6
Outputs:
- output: bfloat16 [16, 512, 768], P('dp', 'tensor')
- tokens_grad: bfloat16 [16, 512, 768], P('dp', 'tensor')
- condition_grad: float32 [16, 768], P('dp', 'tensor')
- gate_logits_grad: float32 [16, 512, 2], P('dp', 'tensor')
- ada_weight_grad: float32 [768, 6, 768], P('dp', None, 'tensor')
- ada_bias_grad: float32 [6, 768], P(None, ('tensor', 'dp'))
- qkv_weight_grad: float32 [768, 3, 768], P('dp', None, 'tensor')
- out_weight_grad: float32 [768, 768], P('dp', 'tensor')
- out_bias_grad: float32 [768], P(('dp', 'tensor'))
- fc1_weight_grad: float32 [768, 3072], P('dp', 'tensor')
- fc1_bias_grad: float32 [3072], P(('tensor', 'dp'))
- fc2_weight_grad: float32 [768, 3072], P('dp', 'tensor')
- fc2_bias_grad: float32 [768], P(('dp', 'tensor'))
- expert_in_grad: float32 [768, 8, 3072], P('dp', None, 'tensor')
- expert_out_grad: float32 [768, 8, 3072], P('dp', None, 'tensor')
Inputs may be any that keep to these rules, and one draw needn't show every extreme that they name: `valid_mask`: each item's real patches are its first 256 or all 512; among items i * 2 to (i + 1) * 2 - 1 at least one is all real. `routes`: the two experts of a patch differ; no expert is named by more than 192 pairs of one item, padded patches included, and some item reaches 192.
All inputs are finite; a program needn't handle non-finite values.
Results may differ from a plain program's by a relative error of at most 0.02.
The roundings to bfloat16 on the way count: a program that leaves them out, or rounds other values in their place, can miss the bound.
Values may be sent and summed in bfloat16 or wider, within the bound.
No kernel may reach another device: no remote copies, remote signals or barrier semaphores. Data moves between devices by JAX's collectives and lax.ppermute only.
A program may use at most 256 MiB of HBM per device.

v0:
```python
import jax
import jax.numpy as jnp
from jax import lax
from jax.sharding import PartitionSpec as P

HD = 64
E = 8
CAP = 192


highest = lax.Precision.HIGHEST


def layer_norm(values):
    center = values - jnp.mean(values, axis=-1, keepdims=True)
    spread = jnp.mean(center * center, axis=-1, keepdims=True)
    return center * lax.rsqrt(spread + 1e-06)


def smooth_gelu(values):
    return jax.nn.gelu(values, approximate=True)


def pair_slots(routes, valid_mask):
    batch_items = routes.shape[0]
    pair_count = routes.shape[1] * 2
    flat_routes = routes.reshape(batch_items, pair_count)
    live_pair = jnp.repeat(valid_mask, 2, axis=1)
    expert_ids = jnp.arange(E, dtype=jnp.int32)
    choose = (
        (flat_routes[:, :, None] == expert_ids[None, None, :]) & (live_pair[:, :, None] > 0)
    ).astype(jnp.int32)
    before = jnp.cumsum(choose, axis=1) - choose
    position = jnp.sum(before * choose, axis=2)
    slot_index = flat_routes * CAP + position
    slot_ids = jnp.arange(E * CAP, dtype=jnp.int32)
    pair_hot = (
        (slot_index[:, :, None] == slot_ids[None, None, :]) & (live_pair[:, :, None] > 0)
    ).astype(jnp.bfloat16)
    return (pair_hot, live_pair)


def exact_spread(slot_map, values):
    upper = values.astype(jnp.bfloat16)
    rest = values - upper.astype(jnp.float32)
    middle_part = rest.astype(jnp.bfloat16)
    lower = (rest - middle_part.astype(jnp.float32)).astype(jnp.bfloat16)
    total = jnp.einsum("isc,icd->isd", slot_map, upper, preferred_element_type=jnp.float32)
    total = total + jnp.einsum(
        "isc,icd->isd", slot_map, middle_part, preferred_element_type=jnp.float32
    )
    return total + jnp.einsum("isc,icd->isd", slot_map, lower, preferred_element_type=jnp.float32)


def attention_scores(normed, qkv_weight, valid_mask):
    batch_items, seq_length, model_width = normed.shape
    local_width = qkv_weight.shape[2]
    local_heads = local_width // HD
    projected = jnp.einsum(
        "isd,dcf->iscf", normed, qkv_weight, preferred_element_type=jnp.float32
    ).astype(jnp.bfloat16)
    queries = projected[:, :, 0].reshape(batch_items, seq_length, local_heads, HD)
    key_rows = projected[:, :, 1].reshape(batch_items, seq_length, local_heads, HD)
    value_rows = projected[:, :, 2].reshape(batch_items, seq_length, local_heads, HD)
    scores = (
        jnp.einsum("ishe,ithe->ihst", queries, key_rows, preferred_element_type=jnp.float32) * 0.125
    )
    scores = jnp.where(valid_mask[:, None, None, :] > 0, scores, -1e30)
    return (queries, key_rows, value_rows, scores)


def body(
    tokens,
    time_embed,
    class_embed,
    valid_mask,
    routes,
    gate_logits,
    ada_weight,
    ada_bias,
    qkv_weight,
    out_weight,
    out_bias,
    fc1_weight,
    fc1_bias,
    fc2_weight,
    fc2_bias,
    expert_in,
    expert_out,
    out_grad,
):
    batch_items, local_length, model_width = tokens.shape
    tensor_size = lax.axis_size("tensor")
    tensor_rank = lax.axis_index("tensor")
    seq_length = local_length * tensor_size
    local_width = qkv_weight.shape[2]
    local_heads = local_width // HD
    local_cols = ada_weight.shape[2]
    start_row = tensor_rank * local_length
    condition = time_embed + class_embed
    cond_wide, silu_pull = jax.vjp(jax.nn.silu, condition)
    cond_low = cond_wide.astype(jnp.bfloat16)
    bias_cols = lax.dynamic_slice_in_dim(ada_bias, tensor_rank * local_cols, local_cols, 1)
    modulation_local = (
        jnp.einsum("id,dsk->isk", cond_low, ada_weight, preferred_element_type=jnp.float32)
        + bias_cols.astype(jnp.float32)[None]
    )
    modulation = lax.all_gather(modulation_local, "tensor", axis=2, tiled=True)
    parts = [modulation[:, column][:, None, :] for column in range(6)]
    shift_attn, scale_attn, gate_attn, shift_mlp, scale_mlp, gate_mlp = parts
    tokens_wide = tokens.astype(jnp.float32)
    norm_attn, norm_attn_pull = jax.vjp(layer_norm, tokens_wide)
    normed_local = (norm_attn * (1.0 + scale_attn) + shift_attn).astype(jnp.bfloat16)
    normed_full = lax.all_gather(normed_local, "tensor", axis=1, tiled=True)
    queries, key_rows, value_rows, scores = attention_scores(normed_full, qkv_weight, valid_mask)
    top_score = jnp.max(scores, axis=-1, keepdims=True)
    exponent = jnp.exp(scores - top_score)
    row_total = jnp.sum(exponent, axis=-1, keepdims=True)
    attn_probs = exponent / row_total
    log_total = top_score + jnp.log(row_total)
    mixed_heads = jnp.einsum(
        "ihst,ithe->ishe",
        attn_probs.astype(jnp.bfloat16),
        value_rows,
        preferred_element_type=jnp.float32,
    )
    mixed_heads = mixed_heads.reshape(batch_items, seq_length, local_width).astype(jnp.bfloat16)
    projected_out = jnp.einsum(
        "isf,df->isd", mixed_heads, out_weight, preferred_element_type=jnp.float32
    )
    attn_sum = lax.psum_scatter(
        projected_out.astype(jnp.bfloat16), "tensor", scatter_dimension=1, tiled=True
    ).astype(jnp.float32)
    branch_attn = attn_sum + out_bias.astype(jnp.float32)
    middle = tokens_wide + gate_attn * branch_attn
    norm_mlp, norm_mlp_pull = jax.vjp(layer_norm, middle)
    normed_mlp_local = (norm_mlp * (1.0 + scale_mlp) + shift_mlp).astype(jnp.bfloat16)
    normed_mlp = lax.all_gather(normed_mlp_local, "tensor", axis=1, tiled=True)
    hidden = jnp.einsum(
        "isd,df->isf", normed_mlp, fc1_weight, preferred_element_type=jnp.float32
    ) + fc1_bias.astype(jnp.float32)
    hidden_wide, gelu_pull = jax.vjp(smooth_gelu, hidden)
    hidden_act = hidden_wide.astype(jnp.bfloat16)
    shared = jnp.einsum("isf,df->isd", hidden_act, fc2_weight, preferred_element_type=jnp.float32)
    pair_hot, live_pair = pair_slots(routes, valid_mask)
    slot_count = E * CAP
    pair_view = pair_hot.reshape(batch_items, seq_length, 2, slot_count)
    slot_map = jnp.sum(pair_view, axis=2, dtype=jnp.float32).astype(jnp.bfloat16)
    live_share = live_pair.reshape(batch_items, seq_length, 2).astype(jnp.float32)
    gate_share = jax.nn.softmax(gate_logits, axis=-1) * live_share
    share_slot = jnp.einsum(
        "isk,iskc->ic", gate_share, pair_view.astype(jnp.float32), precision=highest
    )
    buffer = jnp.einsum(
        "isc,isd->icd", slot_map, normed_mlp, preferred_element_type=jnp.float32
    ).astype(jnp.bfloat16)
    buffer = buffer.reshape(batch_items, E, CAP, model_width)
    upward = jnp.einsum("iecd,def->iecf", buffer, expert_in, preferred_element_type=jnp.float32)
    expert_act = smooth_gelu(upward).astype(jnp.bfloat16)
    returned = jnp.einsum(
        "iecf,def->iecd", expert_act, expert_out, preferred_element_type=jnp.float32
    )
    returned = returned.reshape(batch_items, slot_count, model_width)
    mixture = exact_spread(slot_map, returned * share_slot[:, :, None])
    mlp_sum = lax.psum_scatter(
        (shared + mixture).astype(jnp.bfloat16), "tensor", scatter_dimension=1, tiled=True
    ).astype(jnp.float32)
    branch_mlp = mlp_sum + fc2_bias.astype(jnp.float32)
    output = (middle + gate_mlp * branch_mlp).astype(jnp.bfloat16)
    cotangent = out_grad.astype(jnp.float32)
    gate_mlp_grad = jnp.sum(cotangent * branch_mlp, axis=1)
    branch_mlp_grad = (gate_mlp * cotangent).astype(jnp.bfloat16)
    fc2_bias_part = jnp.sum(branch_mlp_grad.astype(jnp.float32), axis=(0, 1))
    branch_mlp_full = lax.all_gather(branch_mlp_grad, "tensor", axis=1, tiled=True)
    fc2_weight_grad = jnp.einsum(
        "isd,isf->df", branch_mlp_full, hidden_act, preferred_element_type=jnp.float32
    )
    act_grad = jnp.einsum(
        "isd,df->isf", branch_mlp_full, fc2_weight, preferred_element_type=jnp.float32
    )
    hidden_grad = gelu_pull(act_grad)[0].astype(jnp.bfloat16)
    fc1_bias_grad = jnp.sum(hidden_grad.astype(jnp.float32), axis=(0, 1))
    fc1_weight_grad = jnp.einsum(
        "isd,isf->df", normed_mlp, hidden_grad, preferred_element_type=jnp.float32
    )
    normed_mlp_grad = jnp.einsum(
        "isf,df->isd", hidden_grad, fc1_weight, preferred_element_type=jnp.float32
    )
    upward_again = jnp.einsum(
        "iecd,def->iecf", buffer, expert_in, preferred_element_type=jnp.float32
    )
    expert_wide, expert_pull = jax.vjp(smooth_gelu, upward_again)
    expert_again = expert_wide.astype(jnp.bfloat16)
    branch_slot = jnp.einsum(
        "isc,isd->icd", slot_map, branch_mlp_full, preferred_element_type=jnp.float32
    )
    slot_dot = jnp.sum(branch_slot * returned, axis=2)
    gate_grad_part = jnp.einsum(
        "iskc,ic->isk", pair_view.astype(jnp.float32), slot_dot, precision=highest
    )
    returned_grad = (
        (branch_slot * share_slot[:, :, None])
        .reshape(batch_items, E, CAP, model_width)
        .astype(jnp.bfloat16)
    )
    expert_out_grad = jnp.einsum(
        "iecd,iecf->def", returned_grad, expert_again, preferred_element_type=jnp.float32
    )
    expert_act_grad = jnp.einsum(
        "iecd,def->iecf", returned_grad, expert_out, preferred_element_type=jnp.float32
    )
    upward_grad = expert_pull(expert_act_grad)[0].astype(jnp.bfloat16)
    expert_in_grad = jnp.einsum(
        "iecd,iecf->def", buffer, upward_grad, preferred_element_type=jnp.float32
    )
    buffer_grad = jnp.einsum(
        "iecf,def->iecd", upward_grad, expert_in, preferred_element_type=jnp.float32
    )
    buffer_grad = buffer_grad.reshape(batch_items, slot_count, model_width)
    normed_mlp_grad = normed_mlp_grad + exact_spread(slot_map, buffer_grad)
    normed_mlp_local_grad, gate_grad = (
        lax.psum_scatter(
            normed_mlp_grad.astype(jnp.bfloat16), "tensor", scatter_dimension=1, tiled=True
        ).astype(jnp.float32),
        lax.psum_scatter(
            gate_grad_part.astype(jnp.bfloat16), "tensor", scatter_dimension=1, tiled=True
        ).astype(jnp.float32),
    )
    local_logits = lax.dynamic_slice_in_dim(gate_logits, start_row, local_length, 1)
    local_live = lax.dynamic_slice_in_dim(live_share, start_row, local_length, 1)
    soft_local = jax.nn.softmax(local_logits, axis=-1)
    share_grad = gate_grad * local_live
    gate_logits_grad = soft_local * (
        share_grad - jnp.sum(soft_local * share_grad, axis=-1, keepdims=True)
    )
    shift_mlp_grad = jnp.sum(normed_mlp_local_grad, axis=1)
    scale_mlp_grad = jnp.sum(normed_mlp_local_grad * norm_mlp, axis=1)
    middle_grad = cotangent + norm_mlp_pull(normed_mlp_local_grad * (1.0 + scale_mlp))[0]
    gate_attn_grad = jnp.sum(middle_grad * branch_attn, axis=1)
    branch_attn_grad = (gate_attn * middle_grad).astype(jnp.bfloat16)
    out_bias_part = jnp.sum(branch_attn_grad.astype(jnp.float32), axis=(0, 1))
    branch_attn_full = lax.all_gather(branch_attn_grad, "tensor", axis=1, tiled=True)
    queries, key_rows, value_rows, scores = attention_scores(normed_full, qkv_weight, valid_mask)
    attn_probs = jnp.exp(scores - log_total)
    probs_low = attn_probs.astype(jnp.bfloat16)
    mixed_heads = jnp.einsum(
        "ihst,ithe->ishe", probs_low, value_rows, preferred_element_type=jnp.float32
    )
    mixed_heads = mixed_heads.reshape(batch_items, seq_length, local_width).astype(jnp.bfloat16)
    out_weight_grad = jnp.einsum(
        "isd,isf->df", branch_attn_full, mixed_heads, preferred_element_type=jnp.float32
    )
    mixed_grad = jnp.einsum(
        "isd,df->isf", branch_attn_full, out_weight, preferred_element_type=jnp.float32
    )
    mixed_grad = mixed_grad.astype(jnp.bfloat16).reshape(batch_items, seq_length, local_heads, HD)
    value_grad = jnp.einsum(
        "ihst,ishe->ithe", probs_low, mixed_grad, preferred_element_type=jnp.float32
    )
    prob_grad = jnp.einsum(
        "ishe,ithe->ihst", mixed_grad, value_rows, preferred_element_type=jnp.float32
    )
    row_dot = jnp.sum(attn_probs * prob_grad, axis=-1, keepdims=True)
    score_grad = (attn_probs * (prob_grad - row_dot)).astype(jnp.bfloat16)
    query_grad = (
        jnp.einsum("ihst,ithe->ishe", score_grad, key_rows, preferred_element_type=jnp.float32)
        * 0.125
    )
    key_grad = (
        jnp.einsum("ihst,ishe->ithe", score_grad, queries, preferred_element_type=jnp.float32)
        * 0.125
    )
    project_grad = jnp.stack(
        [
            query_grad.reshape(batch_items, seq_length, local_width),
            key_grad.reshape(batch_items, seq_length, local_width),
            value_grad.reshape(batch_items, seq_length, local_width),
        ],
        axis=2,
    ).astype(jnp.bfloat16)
    qkv_weight_grad = jnp.einsum(
        "isd,iscf->dcf", normed_full, project_grad, preferred_element_type=jnp.float32
    )
    normed_attn_grad = jnp.einsum(
        "iscf,dcf->isd", project_grad, qkv_weight, preferred_element_type=jnp.float32
    )
    normed_attn_local_grad = lax.psum_scatter(
        normed_attn_grad.astype(jnp.bfloat16), "tensor", scatter_dimension=1, tiled=True
    ).astype(jnp.float32)
    shift_attn_grad = jnp.sum(normed_attn_local_grad, axis=1)
    scale_attn_grad = jnp.sum(normed_attn_local_grad * norm_attn, axis=1)
    tokens_grad = (
        middle_grad + norm_attn_pull(normed_attn_local_grad * (1.0 + scale_attn))[0]
    ).astype(jnp.bfloat16)
    modulation_part = jnp.stack(
        [
            shift_attn_grad,
            scale_attn_grad,
            gate_attn_grad,
            shift_mlp_grad,
            scale_mlp_grad,
            gate_mlp_grad,
        ],
        axis=1,
    )
    modulation_grad = lax.psum_scatter(
        modulation_part.astype(jnp.bfloat16), "tensor", scatter_dimension=2, tiled=True
    )
    ada_weight_grad = jnp.einsum(
        "id,isk->dsk", cond_low, modulation_grad, preferred_element_type=jnp.float32
    )
    ada_bias_grad = jnp.sum(modulation_grad.astype(jnp.float32), axis=0)
    cond_act_grad = jnp.einsum(
        "isk,dsk->id", modulation_grad, ada_weight, preferred_element_type=jnp.float32
    )
    condition_part = silu_pull(cond_act_grad)[0]
    bias_pair = jnp.stack([out_bias_part, fc2_bias_part], axis=1)
    all_summed = (
        lax.psum_scatter(ada_weight_grad, "dp", scatter_dimension=0, tiled=True),
        lax.psum_scatter(ada_bias_grad.T, "dp", scatter_dimension=0, tiled=True),
        lax.psum_scatter(qkv_weight_grad, "dp", scatter_dimension=0, tiled=True),
        lax.psum_scatter(out_weight_grad, "dp", scatter_dimension=0, tiled=True),
        lax.psum_scatter(bias_pair, "dp", scatter_dimension=0, tiled=True),
        lax.psum_scatter(fc1_weight_grad, "dp", scatter_dimension=0, tiled=True),
        lax.psum_scatter(fc1_bias_grad, "dp", scatter_dimension=0, tiled=True),
        lax.psum_scatter(fc2_weight_grad, "dp", scatter_dimension=0, tiled=True),
        lax.psum_scatter(expert_in_grad, "dp", scatter_dimension=0, tiled=True),
        lax.psum_scatter(expert_out_grad, "dp", scatter_dimension=0, tiled=True),
    )
    (
        ada_weight_sum,
        ada_bias_sum,
        qkv_weight_sum,
        out_weight_sum,
        bias_pair_sum,
        fc1_weight_sum,
        fc1_bias_sum,
        fc2_weight_sum,
        expert_in_sum,
        expert_out_sum,
    ) = all_summed
    condition_grad, bias_final = (
        lax.psum_scatter(condition_part, "tensor", scatter_dimension=1, tiled=True),
        lax.psum_scatter(bias_pair_sum.T, "tensor", scatter_dimension=1, tiled=True),
    )
    return (
        output,
        tokens_grad,
        condition_grad,
        gate_logits_grad,
        ada_weight_sum,
        ada_bias_sum.T,
        qkv_weight_sum,
        out_weight_sum,
        bias_final[0],
        fc1_weight_sum,
        fc1_bias_sum,
        fc2_weight_sum,
        bias_final[1],
        expert_in_sum,
        expert_out_sum,
    )


def solution(mesh):
    in_specs = (
        P("dp", "tensor", None),
        P("dp", None),
        P("dp", None),
        P("dp", None),
        P("dp", None, None),
        P("dp", None, None),
        P(None, None, "tensor"),
        P(),
        P(None, None, "tensor"),
        P(None, "tensor"),
        P(),
        P(None, "tensor"),
        P("tensor"),
        P(None, "tensor"),
        P(),
        P(None, None, "tensor"),
        P(None, None, "tensor"),
        P("dp", "tensor", None),
    )
    out_specs = (
        P("dp", "tensor", None),
        P("dp", "tensor", None),
        P("dp", "tensor"),
        P("dp", "tensor", None),
        P("dp", None, "tensor"),
        P(None, ("tensor", "dp")),
        P("dp", None, "tensor"),
        P("dp", "tensor"),
        P(("dp", "tensor")),
        P("dp", "tensor"),
        P(("tensor", "dp")),
        P("dp", "tensor"),
        P(("dp", "tensor")),
        P("dp", None, "tensor"),
        P("dp", None, "tensor"),
    )
    return jax.shard_map(body, mesh=mesh, in_specs=in_specs, out_specs=out_specs, check_vma=False)
```

profile of v0, /device:TPU:0, one launch (start us, length us, event | category | flops | bytes accessed | tf_op | source)
XLA Modules:
  0.0 1063.3 jit_solution(14763808890003768920)
XLA Ops:
  12.0 21.3 %all_gather.15 = f32[2,6,768]{1,0,2:T(2,128)S(1)} all-gather(f32[2,6,192]{1,0,2:T(2,128)S(1)} %copy.205), channel_id=1, replica_groups=mesh['dp'=8,'tensor'=4] {'tensor'}, dimensions={2}, use_global_device_ids=true | all-gather | bytes 46080 | tf_op jit(solution)/shard_map/all_gather | solution.py:108
  42.6 36.5 %all-gather.5.cloned.1.call-done = bf16[2,512,768]{2,1,0:T(8,128)(2,1)} async-done(((bf16[2,128,768]{2,1,0:T(8,128)(2,1)}), bf16[2,512,768]{2,1,0:T(8,128)(2,1)}) %all-gather.5.cloned.1.call-update) | async-done | bytes 1572880 | tf_op jit(solution)/shard_map/all_gather | solution.py:114
  93.3 30.2 %reduce-scatter.26.cloned.1.call-done = bf16[2,128,768]{2,1,0:T(8,128)(2,1)} async-done(((bf16[2,512,768]{2,1,0:T(8,128)(2,1)}), bf16[2,128,768]{2,1,0:T(8,128)(2,1)}) %reduce-scatter.26.cloned.1.call-update) | async-done | bytes 393232 | tf_op jit(solution)/shard_map/reduce_scatter | solution.py:131
  148.2 16.1 %all-gather.7.cloned.1.call-done = bf16[2,512,768]{2,1,0:T(8,128)(2,1)} async-done(((bf16[2,128,768]{2,1,0:T(8,128)(2,1)}), bf16[2,512,768]{2,1,0:T(8,128)(2,1)}) %all-gather.7.cloned.1.call-update) | async-done | bytes 1572880 | tf_op jit(solution)/shard_map/all_gather | solution.py:138
  169.3 15.0 %fusion.30 = f32[8,2,192,768]{3,2,1,0:T(8,128)} fusion(bf16[768,8,768,1]{2,1,0,3:T(8,128)(2,1)} %bitcast.269, bf16[2,8,192,768]{3,2,1,0:T(8,128)(2,1)S(1)} %bitcast.319), kind=kOutput, calls=%fused_computation.42 | convolution fusion | flops 3623878656 | bytes 23592960 | tf_op jit(solution)/shard_map/iecd,def->iecf/dot_general | solution.py:158
  184.3 15.8 %fusion.50 = f32[2,8,192,768]{3,2,0,1:T(8,128)} fusion(bf16[768,8,768,1]{2,1,0,3:T(8,128)(2,1)} %bitcast.317, f32[8,2,192,768]{3,2,1,0:T(8,128)} %fusion.30), kind=kOutput, calls=%fused_computation.69 | convolution fusion | flops 3645112320 | bytes 28311552 | tf_op jit(solution)/shard_map/iecf,def->iecd/dot_general | solution.py:160
  208.4 11.9 %fusion.40 = (bf16[2,1536,768]{2,1,0:T(8,128)(2,1)}, bf16[2,1536,768]{2,1,0:T(8,128)(2,1)}, bf16[2,1536,768]{2,1,0:T(8,128)(2,1)}, f32[2,1536]{1,0:T(2,128)S(1)}, bf16[2,1536,768]{2,1,0:T(8,128)(2,1)}) fusion(f32[2,8,192,768]{3,2,1,0:T(8,128)} %copy.220, f32[2,1536]{1,0:T(2,128)S(1)} %bitcast.310, bf16[2,512,1536]{2,1,0:T(8,128)(2,1)} %fusion.35, ...), kind=kOutput, calls=%fused_computation.58 | convolution fusion | flops 2444227584 | bytes 33054720 | tf_op jit(solution)/shard_map/isc,isd->icd/dot_general | solution.py:194
  220.3 15.8 %fusion.17 = bf16[2,8,192,768]{3,2,0,1:T(8,128)(2,1)S(1)} fusion(f32[8,2,192,768]{3,2,1,0:T(8,128)} %fusion.30, bf16[768,8,768,1]{2,1,0,3:T(8,128)(2,1)} %bitcast.318, bf16[2,8,192,768]{3,2,1,0:T(8,128)(2,1)} %bitcast.272), kind=kOutput, calls=%fused_computation.18 | convolution fusion | flops 3671064576 | bytes 28311552 | tf_op jit(solution)/shard_map/iecd,def->iecf/dot_general | solution.py:209
  236.1 14.6 %fusion.47 = f32[2,8,192,768]{3,2,0,1:T(8,128)} fusion(bf16[2,8,192,768]{3,2,0,1:T(8,128)(2,1)S(1)} %fusion.17, bf16[768,8,768,1]{2,1,0,3:T(8,128)(2,1)} %bitcast.270), kind=kOutput, calls=%fused_computation.68 | convolution fusion | flops 3623878656 | bytes 23592960 | tf_op jit(solution)/shard_map/iecf,def->iecd/dot_general | solution.py:216
  289.8 34.3 %reduce-scatter.30.cloned.1.call-done = bf16[2,128,768]{2,1,0:T(8,128)(2,1)} async-done(((bf16[2,512,768]{2,1,0:T(8,128)(2,1)}), bf16[2,128,768]{2,1,0:T(8,128)(2,1)}) %reduce-scatter.30.cloned.1.call-update) | async-done | bytes 393232 | tf_op jit(solution)/shard_map/reduce_scatter | solution.py:222
  329.3 36.1 %all-gather.11.cloned.1.call-done = bf16[2,512,768]{2,1,0:T(8,128)(2,1)} async-done(((bf16[2,128,768]{2,1,0:T(8,128)(2,1)}), bf16[2,512,768]{2,1,0:T(8,128)(2,1)}) %all-gather.11.cloned.1.call-update) | async-done | bytes 1572880 | tf_op jit(solution)/shard_map/all_gather | solution.py:242
  402.1 17.0 %reduce-scatter.32.cloned.1.call-done = bf16[2,128,768]{2,1,0:T(8,128)(2,1)} async-done(((bf16[2,512,768]{2,1,0:T(8,128)(2,1)}), bf16[2,128,768]{2,1,0:T(8,128)(2,1)}) %reduce-scatter.32.cloned.1.call-update) | async-done | bytes 393232 | tf_op jit(solution)/shard_map/reduce_scatter | solution.py:287
  421.6 34.7 %reduce-scatter.28.cloned.1.call-done = bf16[2,128,768]{2,1,0:T(8,128)(2,1)} async-done(((bf16[2,512,768]{2,1,0:T(8,128)(2,1)}), bf16[2,128,768]{2,1,0:T(8,128)(2,1)}) %reduce-scatter.28.cloned.1.call-update) | async-done | bytes 393232 | tf_op jit(solution)/shard_map/reduce_scatter | solution.py:165
  509.2 17.0 %convolution_bitcast_fusion = f32[768,8,768]{0,2,1:T(8,128)} fusion(bf16[2,8,192,768]{3,2,1,0:T(8,128)(2,1)} %bitcast.273, f32[8,2,192,768]{3,2,1,0:T(8,128)} %fusion.30), kind=kOutput, calls=%fused_computation.44 | convolution fusion | flops 3645112320 | bytes 33030144 | tf_op jit(solution)/shard_map/iecd,iecf->def/dot_general | solution.py:206
  526.2 19.2 %copy.241 = f32[768,8,768]{2,1,0:T(8,128)} copy(f32[768,8,768]{0,2,1:T(8,128)} %convolution_bitcast_fusion) | data formatting | bytes 37748736 | tf_op jit(solution)/shard_map/iecd,iecf->def/transpose | solution.py:206
  545.7 12.1 %convolution_bitcast_fusion.1 = f32[768,8,768]{0,2,1:T(8,128)} fusion(bf16[2,8,192,768]{3,2,0,1:T(8,128)(2,1)} %copy-done.10, bf16[2,8,192,768]{3,2,1,0:T(8,128)(2,1)} %bitcast.320), kind=kOutput, calls=%fused_computation.45 | convolution fusion | flops 3623878656 | bytes 28311552 | tf_op jit(solution)/shard_map/iecd,iecf->def/dot_general | solution.py:213
  557.8 19.4 %copy.239 = f32[768,8,768]{2,1,0:T(8,128)} copy(f32[768,8,768]{0,2,1:T(8,128)} %convolution_bitcast_fusion.1) | data formatting | bytes 37748736 | tf_op jit(solution)/shard_map/iecd,iecf->def/transpose | solution.py:213
  596.6 22.5 %all-reduce.3 = (f32[192,6]{0,1:T(8,128)S(1)}, f32[768]{0:T(1024)S(1)}) all-reduce(f32[192,6]{0,1:T(8,128)S(1)} %bitcast.311, f32[768]{0:T(1024)S(1)} %get-tuple-element.81), channel_id=10, replica_groups=mesh['dp'=8,'tensor'=4] {'dp'}, use_global_device_ids=true, to_apply=%region_36.37.clone | all-reduce | flops 1920 | bytes 15360
  621.9 29.7 %reduce-scatter.42.cloned.1.call-done = f32[96,768]{1,0:T(8,128)} async-done(((f32[768,768]{1,0:T(8,128)}), f32[96,768]{1,0:T(8,128)}) %reduce-scatter.42.cloned.1.call-update) | async-done | bytes 294928 | tf_op jit(solution)/shard_map/reduce_scatter | solution.py:326
  651.6 38.9 %reduce-scatter.38.cloned.1.call-done = f32[96,192]{1,0:T(8,128)} async-done(((f32[768,192]{1,0:T(8,128)}), f32[96,192]{1,0:T(8,128)}) %reduce-scatter.38.cloned.1.call-update) | async-done | bytes 73744 | tf_op jit(solution)/shard_map/reduce_scatter | solution.py:322
  690.5 46.6 %reduce-scatter.36.cloned.1.call-done = f32[96,3,192]{2,0,1:T(8,128)} async-done(((f32[768,3,192]{2,0,1:T(8,128)}), f32[96,3,192]{2,0,1:T(8,128)}) %reduce-scatter.36.cloned.1.call-update) | async-done | bytes 221200 | tf_op jit(solution)/shard_map/reduce_scatter | solution.py:321
  737.1 57.8 %reduce-scatter.34.cloned.1.call-done = f32[96,6,192]{2,0,1:T(8,128)} async-done(((f32[768,6,192]{2,0,1:T(8,128)}), f32[96,6,192]{2,0,1:T(8,128)}) %reduce-scatter.34.cloned.1.call-update) | async-done | bytes 442384 | tf_op jit(solution)/shard_map/reduce_scatter | solution.py:319
  794.9 130.6 %reduce-scatter.46.cloned.1.call-done = f32[96,8,768]{2,1,0:T(8,128)} async-done(((f32[768,8,768]{2,1,0:T(8,128)}), f32[96,8,768]{2,1,0:T(8,128)}) %reduce-scatter.46.cloned.1.call-update) | async-done | bytes 2359312 | tf_op jit(solution)/shard_map/reduce_scatter | solution.py:328
  925.5 130.8 %reduce-scatter.44.cloned.1.call-done = f32[96,8,768]{2,1,0:T(8,128)} async-done(((f32[768,8,768]{2,1,0:T(8,128)}), f32[96,8,768]{2,1,0:T(8,128)}) %reduce-scatter.44.cloned.1.call-update) | async-done | bytes 2359312 | tf_op jit(solution)/shard_map/reduce_scatter | solution.py:327
  (311 shorter events, 221.6 us)
Async XLA Ops:
  7.2 71.9 %all-gather.5.cloned.1.call-start = ((), (), s32[]{:S(2)}) async-start(), calls=%async_computation.15 | async-start | bytes 1966080 | tf_op jit(solution)/shard_map/all_gather | solution.py:114
  42.5 81.0 %reduce-scatter.26.cloned.1.call-start = ((), (), s32[]{:S(2)}) async-start(), calls=%async_computation.16 | async-start | bytes 1966080 | tf_op jit(solution)/shard_map/reduce_scatter | solution.py:131
  42.5 101.0 %copy-start.34 = (pred[2,512]{1,0:T(4,128)(4,1)}, pred[2,512]{1,0:T(4,128)(4,1)S(1)}, u32[]{:S(2)}) copy-start(pred[2,512]{1,0:T(4,128)(4,1)S(1)} %broadcast_compare_fusion) | copy-start | bytes 3076
  89.2 75.1 %all-gather.7.cloned.1.call-start = ((), (), s32[]{:S(2)}) async-start(), calls=%async_computation.17 | async-start | bytes 1966080 | tf_op jit(solution)/shard_map/all_gather | solution.py:138
  128.1 80.2 %all-gather.9.cloned.1.call-start = ((), (), s32[]{:S(2)}) async-start(), calls=%async_computation.19 | async-start | bytes 1966080 | tf_op jit(solution)/shard_map/all_gather | solution.py:174
  130.0 194.1 %reduce-scatter.30.cloned.1.call-start = ((), (), s32[]{:S(2)}) async-start(), calls=%async_computation.20 | async-start | bytes 1966080 | tf_op jit(solution)/shard_map/reduce_scatter | solution.py:222
  289.7 75.7 %copy-start.27 = (bf16[768,192]{0,1:T(8,128)(2,1)S(1)}, bf16[768,192]{0,1:T(8,128)(2,1)}, u32[]{:S(2)}) copy-start(bf16[768,192]{0,1:T(8,128)(2,1)} %param.27) | copy-start | bytes 884740
  289.7 75.7 %all-gather.11.cloned.1.call-start = ((), (), s32[]{:S(2)}) async-start(), calls=%async_computation.21 | async-start | bytes 1966080 | tf_op jit(solution)/shard_map/all_gather | solution.py:242
  329.2 89.9 %reduce-scatter.32.cloned.1.call-start = ((), (), s32[]{:S(2)}) async-start(), calls=%async_computation.22 | async-start | bytes 1966080 | tf_op jit(solution)/shard_map/reduce_scatter | solution.py:287
  384.8 71.5 %reduce-scatter.28.cloned.1.call-start = ((), (), s32[]{:S(2)}) async-start(), calls=%async_computation.18 | async-start | bytes 1966080 | tf_op jit(solution)/shard_map/reduce_scatter | solution.py:165
  401.9 54.4 %copy-start.33 = (f32[2,1,768]{2,0,1:T(2,128)S(1)}, f32[2,1,768]{2,0,1:T(2,128)}, u32[]{:S(2)}) copy-start(f32[2,1,768]{2,0,1:T(2,128)} %copy-done.32) | copy-start | bytes 18436
  401.9 54.4 %copy-start.42 = (f32[2,128]{1,0:T(2,128)S(1)}, f32[2,128]{1,0:T(2,128)}, u32[]{:S(2)}) copy-start(f32[2,128]{1,0:T(2,128)} %copy-done.41) | copy-start | bytes 3076
  402.0 80.7 %reduce-scatter.48.cloned.1.call-start = ((), (), s32[]{:S(2)}) async-start(), calls=%async_computation.30 | async-start | bytes 245760
  421.5 42.9 %copy-start.35 = (pred[2,512]{1,0:T(4,128)(4,1)S(1)}, pred[2,512]{1,0:T(4,128)(4,1)}, u32[]{:S(2)}) copy-start(pred[2,512]{1,0:T(4,128)(4,1)} %copy-done.34) | copy-start | bytes 3076
  464.2 118.2 %reduce-scatter.52.cloned.1.call-start = ((), (), s32[]{:S(2)}) async-start(), calls=%async_computation.32 | async-start | bytes 163840
  479.0 105.0 %reduce-scatter.54.cloned.1.call-start = ((), (), s32[]{:S(2)}) async-start(), calls=%async_computation.33 | async-start | bytes 442368
  480.0 140.3 %reduce-scatter.50.cloned.1.call-start = ((), (), s32[]{:S(2)}) async-start(), calls=%async_computation.31 | async-start | bytes 491520
  485.4 136.5 %reduce-scatter.40.cloned.1.call-start = ((), (), s32[]{:S(2)}) async-start(), calls=%async_computation.26 | async-start | bytes 2654208 | tf_op jit(solution)/shard_map/reduce_scatter | solution.py:324
  490.2 161.3 %reduce-scatter.42.cloned.1.call-start = ((), (), s32[]{:S(2)}) async-start(), calls=%async_computation.27 | async-start | bytes 2654208 | tf_op jit(solution)/shard_map/reduce_scatter | solution.py:326
  495.8 194.6 %reduce-scatter.38.cloned.1.call-start = ((), (), s32[]{:S(2)}) async-start(), calls=%async_computation.25 | async-start | bytes 884736 | tf_op jit(solution)/shard_map/reduce_scatter | solution.py:322
  501.5 235.6 %reduce-scatter.36.cloned.1.call-start = ((), (), s32[]{:S(2)}) async-start(), calls=%async_computation.24 | async-start | bytes 2654208 | tf_op jit(solution)/shard_map/reduce_scatter | solution.py:321
  506.1 288.8 %reduce-scatter.34.cloned.1.call-start = ((), (), s32[]{:S(2)}) async-start(), calls=%async_computation.23 | async-start | bytes 5308416 | tf_op jit(solution)/shard_map/reduce_scatter | solution.py:319
  509.1 416.4 %reduce-scatter.46.cloned.1.call-start = ((), (), s32[]{:S(2)}) async-start(), calls=%async_computation.29 | async-start | bytes 21233664 | tf_op jit(solution)/shard_map/reduce_scatter | solution.py:328
  545.4 510.9 %reduce-scatter.44.cloned.1.call-start = ((), (), s32[]{:S(2)}) async-start(), calls=%async_computation.28 | async-start | bytes 21233664 | tf_op jit(solution)/shard_map/reduce_scatter | solution.py:327
  (62 other events, 633.9 us)
Sparse Core Ops, SparseCore 0:
  42.6 36.4 all-gather.4
  89.3 34.1 reduce-scatter.25
  128.2 36.0 all-gather.6
  166.3 36.0 all-gather.8
  289.8 34.2 reduce-scatter.29
  329.3 36.0 all-gather.10
  384.9 34.1 reduce-scatter.31
  422.0 34.2 reduce-scatter.27
  464.3 18.2 reduce-scatter.47
  484.9 17.3 reduce-scatter.51
  505.3 32.0 reduce-scatter.53
  539.5 20.5 reduce-scatter.49
  564.4 40.8 reduce-scatter.39
  609.1 42.3 reduce-scatter.41
  655.5 34.9 reduce-scatter.37
  694.6 42.4 reduce-scatter.35
  741.0 53.8 reduce-scatter.33
  799.4 126.0 reduce-scatter.45
  930.1 126.0 reduce-scatter.43
where the time goes:
time: 1070 us; the launch traced here: 1060 us
  waiting for transfers between devices  642 us (60%)
  matrix products  201 us (19%)
  local copies, waits for them, and re-layouts  98.5 us (9%)
  blocking collectives  52.4 us (5%)
  other arithmetic  49.6 us (5%)
  between operations  17.5 us (2%)
    reduce_scatter x1, waiting for transfers between devices, body(): lax.psum_scatter(expert_in_grad, 'dp', scatter_dimension=0, tiled=True)  131 us
    reduce_scatter x1, waiting for transfers between devices, body(): lax.psum_scatter(expert_out_grad, 'dp', scatter_dimension=0, tiled=True)  131 us
    reduce_scatter x1, waiting for transfers between devices, body(): lax.psum_scatter(ada_weight_grad, 'dp', scatter_dimension=0, tiled=True)  57.8 us
    reduce_scatter x1, waiting for transfers between devices, body(): lax.psum_scatter(qkv_weight_grad, 'dp', scatter_dimension=0, tiled=True)  46.6 us
    reduce_scatter x1, waiting for transfers between devices, body(): lax.psum_scatter(out_weight_grad, 'dp', scatter_dimension=0, tiled=True)  38.9 us
    all_gather x1, waiting for transfers between devices, body(): normed_full = lax.all_gather(normed_local, 'tensor', axis=1, tiled=True)  36.5 us
    all_gather x1, waiting for transfers between devices, body(): lax.all_gather(branch_attn_grad, 'tensor', axis=1, tiled=True)  36.1 us
    reduce_scatter x1, waiting for transfers between devices, body(): lax.psum_scatter((shared + mixture).astype(jnp.bfloat16), 'tensor', scatt...  34.7 us
  transfers between devices with their start and end apart: 19, of which 14 were waited for; matrix products, arithmetic and copies ran while one was open for 19% of the time, Pallas kernels for 0%

commit v1 on v0

v1 whole, which is shorter than its diff:
```python
import functools

import jax
import jax.numpy as jnp
from jax import lax
from jax.experimental import pallas as pl
from jax.experimental.pallas import tpu as pltpu
from jax.sharding import PartitionSpec as P

HD = 64
E = 8
CAP = 192
F32 = jnp.float32
BF16 = jnp.bfloat16
I32 = jnp.int32
VMEM_BYTES = 56 * 1024 * 1024


def dot(spec, left, right):
    return jnp.einsum(spec, left, right, preferred_element_type=F32)


def mm(left, right):
    return jnp.dot(left, right, preferred_element_type=F32)


def mm_nt(left, right):
    return lax.dot_general(left, right, (((1,), (1,)), ((), ())), preferred_element_type=F32)


def mm_tn(left, right):
    return lax.dot_general(left, right, (((0,), (0,)), ((), ())), preferred_element_type=F32)


def after(values, *others):
    return lax.optimization_barrier((values,) + others)[0]


def from_rank(values, step):
    size = lax.axis_size("tensor")
    return lax.ppermute(values, "tensor", [(i, (i - step) % size) for i in range(size)])


def to_rank(values, step):
    size = lax.axis_size("tensor")
    return lax.ppermute(values, "tensor", [(i, (i + step) % size) for i in range(size)])


def gather_parts(values):
    size = lax.axis_size("tensor")
    return [values] + [from_rank(values, step) for step in range(1, size)]


def scatter_sum(parts):
    total = parts[0].astype(F32)
    for step in range(1, len(parts)):
        total = total + to_rank(parts[step], step).astype(F32)
    return total


def swing(values, amount, axis):
    twice = jnp.concatenate([values, values], axis=axis)
    return lax.dynamic_slice_in_dim(twice, amount, values.shape[axis], axis)


def dp_exchange(values, bit):
    size = lax.axis_size("dp")
    return lax.ppermute(values, "dp", [(i, i ^ (1 << bit)) for i in range(size)])


def to_relative(blocks):
    size = lax.axis_size("dp")
    rank = lax.axis_index("dp")
    for bit in range(size.bit_length() - 1):
        paired = blocks.reshape((size >> (bit + 1), 2, 1 << bit) + blocks.shape[1:])
        swapped = jnp.where(((rank >> bit) & 1) == 0, paired, paired[:, ::-1])
        blocks = swapped.reshape(blocks.shape)
    return blocks


def dp_scatter(blocks, order, kind):
    current = blocks.reshape((2,) * len(order) + blocks.shape[1:])
    left = sorted(order, reverse=True)
    for bit in order:
        axis = left.index(bit)
        keep = lax.index_in_dim(current, 0, axis, keepdims=False)
        send = lax.index_in_dim(current, 1, axis, keepdims=False)
        other = dp_exchange(send, bit)
        current = (keep.astype(F32) + other.astype(F32)).astype(kind)
        left.pop(axis)
    return current


def dp_gather(values):
    size = lax.axis_size("dp")
    rank = lax.axis_index("dp")
    current = values[None]
    for bit in range(size.bit_length() - 1):
        other = dp_exchange(current, bit)
        mine = (rank >> bit) & 1
        low = jnp.where(mine == 0, current, other)
        high = jnp.where(mine == 0, other, current)
        current = jnp.concatenate([low, high], axis=0)
    return current


def norm_parts(values):
    center = values - jnp.mean(values, axis=-1, keepdims=True)
    spread = jnp.mean(center * center, axis=-1, keepdims=True)
    scale = lax.rsqrt(spread + 1e-06)
    return center * scale, scale


def norm_pull(normed, scale, grad):
    return scale * (
        grad
        - jnp.mean(grad, axis=-1, keepdims=True)
        - normed * jnp.mean(grad * normed, axis=-1, keepdims=True)
    )


def gelu_both(values):
    factor = 0.7978845608028654
    square = values * values
    inner = jnp.tanh(values * (factor + (factor * 0.044715) * square))
    half = 0.5 + 0.5 * inner
    slope = half + values * (half * (1.0 - inner)) * (factor + (factor * 0.134145) * square)
    return values * half, slope


def call(kernel, out_shape, in_specs, out_specs, args, grid=(), scratch=(), flops=0, moved=0, name=None, alias=None):
    return pl.pallas_call(
        kernel,
        out_shape=out_shape,
        grid=grid,
        in_specs=in_specs,
        out_specs=out_specs,
        scratch_shapes=scratch,
        input_output_aliases=alias or {},
        compiler_params=pltpu.CompilerParams(
            vmem_limit_bytes=VMEM_BYTES, dimension_semantics=("arbitrary",) * len(grid)
        ),
        cost_estimate=pl.CostEstimate(flops=flops, bytes_accessed=moved, transcendentals=0),
        name=name,
    )(*args)


def whole(shape):
    zeros = (0,) * len(shape)
    return pl.BlockSpec(shape, lambda *_: zeros)


def shaped(shape, kind):
    return jax.ShapeDtypeStruct(shape, kind)


def pack_heads(values):
    half = values.shape[0] // 2
    rest = jnp.concatenate([values[:half, 128:], values[half:, 128:]], axis=1)
    return jnp.concatenate([values[:, :128], rest], axis=0)


def unpack_heads(values):
    half = values.shape[0] // 3
    rest = values[2 * half :]
    upper = jnp.concatenate([values[:half], rest[:, :64]], axis=1)
    lower = jnp.concatenate([values[half : 2 * half], rest[:, 64:]], axis=1)
    return jnp.concatenate([upper, lower], axis=0)


def attention_kernel(heads, tokens_ref, mod_ref, weight_ref, valid_ref, projected_ref, mixed_ref):
    width = heads * HD
    normed, _ = norm_parts(tokens_ref[0].astype(F32))
    normed = normed * (1.0 + mod_ref[0, 1:2]) + mod_ref[0, 0:1]
    projected = mm(normed.astype(BF16), weight_ref[...]).astype(BF16)
    projected_ref[0] = projected
    live = valid_ref[0] > 0
    mixed = []
    for head in range(heads):
        low = head * HD
        query = projected[:, low : low + HD] * jnp.asarray(0.125, BF16)
        key = projected[:, width + low : width + low + HD]
        value = projected[:, 2 * width + low : 2 * width + low + HD]
        scores = jnp.where(live, mm_nt(query, key), -1e30)
        exponent = jnp.exp(scores - jnp.max(scores, axis=1, keepdims=True))
        probs = exponent * (1.0 / jnp.sum(exponent, axis=1, keepdims=True))
        mixed.append(mm(probs.astype(BF16), value))
    mixed_ref[0] = pack_heads(jnp.concatenate(mixed, axis=1).astype(BF16))


def attention(tokens, mod, weight, valid):
    items, length, width = tokens.shape
    head_width = weight.shape[1] // 3
    return call(
        functools.partial(attention_kernel, head_width // HD),
        (shaped((items, length, 3 * head_width), BF16), shaped((items, 3 * length // 2, 128), BF16)),
        [
            pl.BlockSpec((1, length, width), lambda i: (i, 0, 0)),
            pl.BlockSpec((1, 6, width), lambda i: (i, 0, 0)),
            whole(weight.shape),
            pl.BlockSpec((1, 1, length), lambda i: (i, 0, 0)),
        ],
        (
            pl.BlockSpec((1, length, 3 * head_width), lambda i: (i, 0, 0)),
            pl.BlockSpec((1, 3 * length // 2, 128), lambda i: (i, 0, 0)),
        ),
        (tokens, mod, weight, valid),
        grid=(items,),
        flops=8_000_000_000,
        moved=6_000_000,
        name="attention_forward",
    )


def middle_kernel(ranks, mixed_ref, rest_ref, weight_ref, bias_ref, tokens_ref, mod_ref, middle_ref, branch_ref, normed_ref):
    upper = pl.program_id(1) == 0
    branch = bias_ref[...].astype(F32)
    for rank in range(ranks):
        rest = jnp.where(upper, rest_ref[rank, 0, :, :64], rest_ref[rank, 0, :, 64:])
        branch = branch + mm(jnp.concatenate([mixed_ref[rank, 0], rest], axis=1), weight_ref[rank])
    middle = tokens_ref[0].astype(F32) + mod_ref[0, 2:3] * branch
    middle_ref[0] = middle
    branch_ref[0] = branch.astype(BF16)
    normed, _ = norm_parts(middle)
    normed_ref[0] = (normed * (1.0 + mod_ref[0, 4:5]) + mod_ref[0, 3:4]).astype(BF16)


def middle_part(mixed, weight, bias, tokens, mod):
    items, length, width = tokens.shape
    ranks = mixed.shape[0]
    block = length // 2
    rows = pl.BlockSpec((1, block, width), lambda i, r: (i, r, 0))
    return call(
        functools.partial(middle_kernel, ranks),
        (
            shaped(tokens.shape, F32),
            shaped(tokens.shape, BF16),
            shaped(tokens.shape, BF16),
        ),
        [
            pl.BlockSpec((ranks, 1, block, 128), lambda i, r: (0, i, r, 0)),
            pl.BlockSpec((ranks, 1, block, 128), lambda i, r: (0, i, 2, 0)),
            whole(weight.shape),
            whole(bias.shape),
            rows,
            pl.BlockSpec((1, 6, width), lambda i, r: (i, 0, 0)),
        ],
        (rows, rows, rows),
        (mixed, mixed, weight, bias, tokens, mod),
        grid=(items, 2),
        flops=3_000_000_000,
        moved=12_000_000,
        name="middle",
    )


def hot_rows(expert, marks):
    slots = lax.broadcasted_iota(I32, (CAP, marks.shape[1]), 0) + expert * CAP
    return slots == marks[0:1], slots == marks[1:2]


def as_hot(mask):
    return jnp.where(mask, 1.0, 0.0).astype(BF16)


def forward_kernel(
    items,
    normed_ref,
    marks_ref,
    share_ref,
    columns_ref,
    fc1_ref,
    bias_ref,
    fc2_ref,
    first_ref,
    second_ref,
    buffer_ref,
    act_ref,
    slope_ref,
    hidden_ref,
    hidden_slope_ref,
    out_ref,
    slots_ref,
):
    expert = pl.program_id(0)
    length = normed_ref.shape[1]

    @pl.when(expert == 0)
    def _():
        for item in range(items):
            hidden = mm(normed_ref[item], fc1_ref[...]) + bias_ref[...].astype(F32)
            value, slope = gelu_both(hidden)
            hidden_ref[item] = value.astype(BF16)
            hidden_slope_ref[item] = slope.astype(BF16)

    shares = []
    for item in range(items):
        one, two = hot_rows(expert, marks_ref[item])
        buffer_ref[0, item * CAP : (item + 1) * CAP] = mm(as_hot(one | two), normed_ref[item]).astype(BF16)
        held = jnp.where(one, share_ref[item, 0:1], 0.0) + jnp.where(two, share_ref[item, 1:2], 0.0)
        shares.append(jnp.sum(held, axis=1, keepdims=True))
    share = jnp.concatenate(shares, axis=0)
    value, slope = gelu_both(mm(buffer_ref[0], first_ref[0]))
    act_ref[0] = (share * value).astype(BF16)
    slope_ref[0] = (share * slope).astype(BF16)
    returned = mm_nt(act_ref[0], second_ref[0]).astype(BF16)
    place = pl.ds(pl.multiple_of(expert * CAP, 64), CAP)
    for item in range(items):
        slots_ref[item, place] = returned[item * CAP : (item + 1) * CAP]

    @pl.when(expert == E - 1)
    def _():
        lanes = lax.broadcasted_iota(I32, (length, E * CAP), 1)
        for item in range(items):
            marks = columns_ref[item]
            hot = as_hot((lanes == marks[:, 0:1]) | (lanes == marks[:, 1:2]))
            total = mm(hot, slots_ref[item]) + mm_nt(hidden_ref[item], fc2_ref[...])
            out_ref[item] = total.astype(BF16)


def forward_part(normed, marks, share, columns, fc1, bias, fc2, first, second):
    items, length, width = normed.shape
    units = fc1.shape[1]
    slots = items * CAP
    inner = pl.BlockSpec((1, slots, units), lambda e: (e, 0, 0))
    weight = pl.BlockSpec((1, width, units), lambda e: (e, 0, 0))
    hidden = (items, length, units)
    return call(
        functools.partial(forward_kernel, items),
        (
            shaped((E, slots, width), BF16),
            shaped((E, slots, units), BF16),
            shaped((E, slots, units), BF16),
            shaped(hidden, BF16),
            shaped(hidden, BF16),
            shaped(normed.shape, BF16),
        ),
        [
            whole(normed.shape),
            whole(marks.shape),
            whole(share.shape),
            whole(columns.shape),
            whole(fc1.shape),
            whole(bias.shape),
            whole(fc2.shape),
            weight,
            weight,
        ],
        (
            pl.BlockSpec((1, slots, width), lambda e: (e, 0, 0)),
            inner,
            inner,
            whole(hidden),
            whole(hidden),
            whole(normed.shape),
        ),
        (normed, marks, share, columns, fc1, bias, fc2, first, second),
        grid=(E,),
        scratch=[pltpu.VMEM((items, E * CAP, width), BF16)],
        flops=14_000_000_000,
        moved=40_000_000,
        name="mlp_forward",
    )


def store_blocks(keep_ref, send_ref, rank, index, grad):
    blocks, rows = 2 * keep_ref.shape[0], keep_ref.shape[2]
    for pair in range(blocks // 2):
        place = lax.bitwise_xor(rank // 2, pair)
        low = grad[2 * pair * rows : (2 * pair + 1) * rows]
        high = grad[(2 * pair + 1) * rows : (2 * pair + 2) * rows]
        odd = rank % 2 == 1

        @pl.when(odd)
        def _():
            keep_ref[place, index] = high
            send_ref[place, index] = low

        @pl.when(jnp.logical_not(odd))
        def _():
            keep_ref[place, index] = low
            send_ref[place, index] = high


def split_blocks(grads, dp_size):
    count, width, units = grads.shape
    blocks = to_relative(grads.reshape(count, dp_size, width // dp_size, units).swapaxes(0, 1))
    pairs = blocks.reshape((dp_size // 2, 2) + blocks.shape[1:])
    return pairs[:, 0], pairs[:, 1]


def call_grads(kernel, steps, rank, dp_size, shape, outs, out_specs, specs, args, alias=None):
    width, units = shape
    rows = width // dp_size
    smooth = rows % 16 == 0
    block = pl.BlockSpec((dp_size // 2, 1, rows, units), lambda e: (0, e, 0, 0))
    part = shaped((dp_size // 2, steps, rows, units), BF16)
    return call(
        kernel,
        outs + ((part, part) if smooth else ()),
        [pl.BlockSpec(memory_space=pltpu.SMEM)] + specs,
        out_specs + ((block, block) if smooth else ()),
        (rank,) + args,
        grid=(steps,),
        flops=5_000_000_000,
        moved=20_000_000,
        name="weight_grads",
        alias=alias,
    )


def expert_block(start, count, shape):
    return pl.BlockSpec((1,) + shape, lambda e: (jnp.minimum(e, count - 1) + start, 0, 0))


def slots_kernel(items, start, count, rank_ref, marks_ref, act_ref, *refs):
    expert = pl.program_id(0)
    if start == 0:
        grad_ref, mod_ref, hidden_ref, branch_ref, slots_ref, *grad_refs = refs

        @pl.when(expert == 0)
        def _():
            for item in range(items):
                branch_ref[item] = (grad_ref[item].astype(F32) * mod_ref[item, 5:6]).astype(BF16)

    else:
        branch_ref, _, slots_ref, *grad_refs = refs

    @pl.when(expert < count)
    def _():
        for item in range(items):
            one, two = hot_rows(expert + start, marks_ref[item])
            slots_ref[0, item * CAP : (item + 1) * CAP] = mm(as_hot(one | two), branch_ref[item]).astype(BF16)
        if grad_refs:
            store_blocks(*grad_refs, rank_ref[0], 0, mm_tn(slots_ref[0], act_ref[0]).astype(BF16))

    if start == 0 and grad_refs:

        @pl.when(expert == count)
        def _():
            total = mm_tn(branch_ref[0], hidden_ref[0])
            for item in range(1, items):
                total = total + mm_tn(branch_ref[item], hidden_ref[item])
            store_blocks(*grad_refs, rank_ref[0], 0, total.astype(BF16))


def slots_part(start, count, marks, act, rank, dp_size, grad=None, mod=None, hidden=None, branch=None, held=None):
    items, length, width = (branch if grad is None else grad).shape
    units = act.shape[2]
    slots = items * CAP
    all_rows = whole((items, length, width))
    each = expert_block(start, count, (slots, width))
    filled = shaped((E, slots, width), BF16)
    if start == 0:
        specs, more = [all_rows, whole(mod.shape), whole(hidden.shape)], (grad, mod, hidden)
        outs, out_specs, alias = (shaped(grad.shape, BF16), filled), (all_rows, each), {}
    else:
        specs, more = [all_rows, pl.BlockSpec(memory_space=pl.ANY)], (branch, held)
        outs, out_specs, alias = (filled,), (each,), {4: 0}
    result = call_grads(
        functools.partial(slots_kernel, items, start, count),
        count + (start == 0),
        rank,
        dp_size,
        (width, units),
        outs,
        out_specs,
        [whole(marks.shape), expert_block(start, count, (slots, units))] + specs,
        (marks, act) + more,
        alias,
    )
    if (width // dp_size) % 16:
        picked = slice(start, start + count)
        grads = dot("ecd,ecf->edf", result[-1][picked], act[picked])
        if start == 0:
            grads = jnp.concatenate([grads, dot("isd,isf->df", result[0], hidden)[None]], axis=0)
        result = tuple(result) + split_blocks(grads.astype(BF16), dp_size)
    return result


def dense_right(packed, right_ref, item):
    if not packed:
        return right_ref[item]
    return jnp.concatenate([unpack_heads(right_ref[rank, item]) for rank in range(right_ref.shape[0])], axis=1)


def first_kernel(count, packed, rank_ref, left_ref, right_ref, dense_left_ref, dense_right_ref, *grad_refs):
    expert = pl.program_id(0)

    @pl.when(expert < count)
    def _():
        store_blocks(*grad_refs, rank_ref[0], 0, mm_tn(left_ref[0], right_ref[0]).astype(BF16))

    @pl.when(expert == count)
    def _():
        total = mm_tn(dense_left_ref[0], dense_right(packed, dense_right_ref, 0))
        for item in range(1, dense_left_ref.shape[0]):
            total = total + mm_tn(dense_left_ref[item], dense_right(packed, dense_right_ref, item))
        store_blocks(*grad_refs, rank_ref[0], 0, total.astype(BF16))


def first_part(start, count, left, right, dense, packed, rank, dp_size):
    _, slots, width = left.shape
    units = right.shape[2]
    rows = width // dp_size
    if rows % 16:
        picked = slice(start, start + count)
        items = dense[0].shape[0]
        extra = sum(mm_tn(dense[0][item], dense_right(packed, dense[1], item)) for item in range(items))
        grads = jnp.concatenate([dot("ecd,ecf->edf", left[picked], right[picked]), extra[None]], axis=0)
        return split_blocks(grads.astype(BF16), dp_size)
    return call_grads(
        functools.partial(first_kernel, count, packed),
        count + 1,
        rank,
        dp_size,
        (width, units),
        (),
        (),
        [
            expert_block(start, count, (slots, width)),
            expert_block(start, count, (slots, units)),
            whole(dense[0].shape),
            whole(dense[1].shape),
        ],
        (left, right) + tuple(dense),
    )


def halve_kernel(first, keep_ref, other_ref, kept_ref, sent_ref):
    total = (keep_ref[...].astype(F32) + other_ref[...].astype(F32)).astype(BF16)
    kept_ref[...] = total[0:1] if first else total[:, 0:1]
    sent_ref[...] = total[1:2] if first else total[:, 1:2]


def halve(keep, other, axis):
    lead = keep.shape[0]
    rest = keep.shape[1:]
    zeros = (0,) * len(rest)
    if lead == 2:
        shape, outer, axis = (2, 1) + rest, 1, 0
    else:
        shape, outer = (2, lead // 2) + rest, lead // 2
    if axis == 0:
        block, result = (2, 1) + rest, (1, outer) + rest
        spec = pl.BlockSpec(block, lambda i: (0, i) + zeros)
        out = pl.BlockSpec((1, 1) + rest, lambda i: (0, i) + zeros)
        steps = outer
    else:
        block, result = (1, 2) + rest, (2, 1) + rest
        spec = pl.BlockSpec(block, lambda i: (i, 0) + zeros)
        out = pl.BlockSpec((1, 1) + rest, lambda i: (i, 0) + zeros)
        steps = 2
    size = keep.size * 2
    kept, sent = call(
        functools.partial(halve_kernel, axis == 0),
        (shaped(result, BF16),) * 2,
        [spec, spec],
        (out, out),
        (keep.reshape(shape), other.reshape(shape)),
        grid=(steps,),
        flops=size,
        moved=3 * size,
        name="halve",
    )
    return kept.reshape((lead // 2,) + rest), sent.reshape((lead // 2,) + rest)


def last_kernel(halfway, counts, *refs):
    inputs, (out_ref, *dense_refs) = refs[: 2 * len(counts)], refs[2 * len(counts) :]
    dense = iter(dense_refs)
    place = 0
    for group, size in enumerate(counts):
        keep_ref, other_ref = inputs[2 * group], inputs[2 * group + 1]
        for index in range(size):
            total = keep_ref[index].astype(F32) + other_ref[index].astype(F32)
            if index < halfway:
                out_ref[:, place] = total
                place += 1
            else:
                next(dense)[...] = total


def last(pairs, halfway):
    counts = [keep.shape[0] for keep, _ in pairs]
    rows, units = pairs[0][0].shape[1:]
    args = [value for pair in pairs for value in pair]
    vmem = pl.BlockSpec(memory_space=pltpu.VMEM)
    extra = sum(size > halfway for size in counts)
    return call(
        functools.partial(last_kernel, halfway, counts),
        (shaped((rows, halfway * len(counts), units), F32),) + (shaped((rows, units), F32),) * extra,
        [vmem] * len(args),
        (vmem,) * (1 + extra),
        tuple(args),
        flops=sum(counts) * rows * units,
        moved=8 * sum(counts) * rows * units,
        name="last_sum",
    )


def back_kernel(
    items,
    branch_ref,
    columns_ref,
    fc1_ref,
    fc2_ref,
    hidden_slope_ref,
    slots_ref,
    act_ref,
    slope_ref,
    first_ref,
    second_ref,
    up_grad_ref,
    hidden_grad_ref,
    bias_grad_ref,
    grad_ref,
    gate_ref,
    held_ref,
    dots_ref,
):
    expert = pl.program_id(0)
    length = branch_ref.shape[1]

    @pl.when(expert == 0)
    def _():
        total = jnp.zeros(bias_grad_ref.shape, F32)
        for item in range(items):
            grad = mm(branch_ref[item], fc2_ref[...]) * hidden_slope_ref[item].astype(F32)
            grad = grad.astype(BF16)
            hidden_grad_ref[item] = grad
            total = total + jnp.sum(grad.astype(F32), axis=0, keepdims=True)
            grad_ref[item] = mm_nt(grad, fc1_ref[...])
        bias_grad_ref[...] = total

    pulled = mm(slots_ref[0], second_ref[0])
    up_grad = (pulled * slope_ref[0].astype(F32)).astype(BF16)
    up_grad_ref[0] = up_grad
    total = jnp.sum(act_ref[0].astype(F32) * pulled, axis=1, keepdims=True)
    high = total.astype(BF16).astype(F32)
    lane = lax.broadcasted_iota(I32, (items * CAP, 128), 1)
    split = jnp.where(lane == 0, high, jnp.where(lane == 1, total - high, 0.0)).astype(BF16)
    back = mm_nt(up_grad, first_ref[0]).astype(BF16)
    place = pl.ds(pl.multiple_of(expert * CAP, 64), CAP)
    for item in range(items):
        held_ref[item, place] = back[item * CAP : (item + 1) * CAP]
        dots_ref[item, place] = split[item * CAP : (item + 1) * CAP]

    @pl.when(expert == E - 1)
    def _():
        lanes = lax.broadcasted_iota(I32, (length, E * CAP), 1)
        for item in range(items):
            marks = columns_ref[item]
            one = lanes == marks[:, 0:1]
            two = lanes == marks[:, 1:2]
            grad_ref[item] += mm(as_hot(one | two), held_ref[item])
            gate_ref[item, 0] = mm(as_hot(one), dots_ref[item])
            gate_ref[item, 1] = mm(as_hot(two), dots_ref[item])


def back_part(branch, columns, fc1, fc2, hidden_slope, branch_slot, act, slope, first, second):
    items, length, width = branch.shape
    units = fc1.shape[1]
    slots = items * CAP
    inner = pl.BlockSpec((1, slots, units), lambda e: (e, 0, 0))
    weight = pl.BlockSpec((1, width, units), lambda e: (e, 0, 0))
    hidden = (items, length, units)
    return call(
        functools.partial(back_kernel, items),
        (
            shaped((E, slots, units), BF16),
            shaped(hidden, BF16),
            shaped((1, units), F32),
            shaped(branch.shape, F32),
            shaped((items, 2, length, 128), F32),
        ),
        [
            whole(branch.shape),
            whole(columns.shape),
            whole(fc1.shape),
            whole(fc2.shape),
            whole(hidden),
            pl.BlockSpec((1, slots, width), lambda e: (e, 0, 0)),
            inner,
            inner,
            weight,
            weight,
        ],
        (
            inner,
            whole(hidden),
            whole((1, units)),
            whole(branch.shape),
            whole((items, 2, length, 128)),
        ),
        (branch, columns, fc1, fc2, hidden_slope, branch_slot, act, slope, first, second),
        grid=(E,),
        scratch=[
            pltpu.VMEM((items, E * CAP, width), BF16),
            pltpu.VMEM((items, E * CAP, 128), BF16),
        ],
        flops=12_000_000_000,
        moved=40_000_000,
        name="mlp_back",
    )


def second_norm_kernel(
    ranks, grad_ref, middle_ref, branch_ref, cotangent_ref, mlp_ref, mod_ref, weight_ref, own_ref, middle_grad_ref, low_ref, mixed_ref, sums_ref
):
    step = pl.program_id(1)
    normed, scale = norm_parts(middle_ref[0])
    grad = grad_ref[0]
    block = grad.shape[0]
    shift_sum = jnp.sum(grad, axis=0, keepdims=True)
    scale_sum = jnp.sum(grad * normed, axis=0, keepdims=True)
    pulled = norm_pull(normed, scale, grad * (1.0 + mod_ref[0, 4:5]))
    place = lax.broadcasted_iota(I32, (block, 1), 0) + step * block
    own = (place >= own_ref[0]) & (place < own_ref[1])
    cotangent = cotangent_ref[0].astype(F32)
    mlp_sum = jnp.sum(cotangent * mlp_ref[0].astype(F32), axis=0, keepdims=True)
    pulled = pulled + jnp.where(own, cotangent, 0.0)
    middle_grad_ref[0] = pulled.astype(BF16)
    gate_sum = jnp.sum(pulled * branch_ref[0].astype(F32), axis=0, keepdims=True)
    low = (pulled * mod_ref[0, 2:3]).astype(BF16)
    low_ref[0] = low
    bias_sum = jnp.sum(low.astype(F32), axis=0, keepdims=True)
    for rank in range(ranks):
        mixed = mm_nt(low, weight_ref[rank]).astype(BF16)
        mixed_ref[rank, 0, pl.ds(pl.multiple_of(step * block, 128), block)] = mixed[:, :128]

        @pl.when(step == 0)
        def _():
            mixed_ref[rank, 0, 2 * block :, :64] = mixed[:, 128:]

        @pl.when(step > 0)
        def _():
            mixed_ref[rank, 0, 2 * block :, 64:] = mixed[:, 128:]

    sums = jnp.concatenate([shift_sum, scale_sum, gate_sum, bias_sum, mlp_sum], axis=0)

    @pl.when(step == 0)
    def _():
        sums_ref[0] = sums

    @pl.when(step > 0)
    def _():
        sums_ref[0] += sums


def second_norm_part(grad, middle, branch, cotangent, mlp, mod, weight, own):
    items, length, width = grad.shape
    ranks = weight.shape[0]
    block = length // 2
    rows = pl.BlockSpec((1, block, width), lambda i, r: (i, r, 0))
    return call(
        functools.partial(second_norm_kernel, ranks),
        (
            shaped(grad.shape, BF16),
            shaped(grad.shape, BF16),
            shaped((ranks, items, 3 * length // 2, 128), BF16),
            shaped((items, 5, width), F32),
        ),
        [
            rows,
            rows,
            rows,
            rows,
            rows,
            pl.BlockSpec((1, 6, width), lambda i, r: (i, 0, 0)),
            whole(weight.shape),
            pl.BlockSpec(memory_space=pltpu.SMEM),
        ],
        (
            rows,
            rows,
            pl.BlockSpec((ranks, 1, 3 * length // 2, 128), lambda i, r: (0, i, 0, 0)),
            pl.BlockSpec((1, 5, width), lambda i, r: (i, 0, 0)),
        ),
        (grad, middle, branch, cotangent, mlp, mod, weight, own),
        grid=(items, 2),
        flops=3_000_000_000,
        moved=15_000_000,
        name="second_norm_back",
    )


def attention_back_kernel(
    heads, rank_ref, tokens_ref, mod_ref, weight_ref, valid_ref, projected_ref, mixed_ref, middle_ref, part_ref, sums_ref, *rest
):
    *grad_refs, total_ref = rest
    item = pl.program_id(0)
    width = heads * HD
    base, scale = norm_parts(tokens_ref[0].astype(F32))
    normed = (base * (1.0 + mod_ref[0, 1:2]) + mod_ref[0, 0:1]).astype(BF16)
    projected = projected_ref[0]
    grads = [[], [], []]
    live = valid_ref[0] > 0
    mixed_grad = unpack_heads(mixed_ref[0])
    for head in range(heads):
        low = head * HD
        query = projected[:, low : low + HD] * jnp.asarray(0.125, BF16)
        key = projected[:, width + low : width + low + HD]
        value = projected[:, 2 * width + low : 2 * width + low + HD]
        mixed = mixed_grad[:, low : low + HD]
        scores = jnp.where(live, mm_nt(key, query), -1e30)
        exponent = jnp.exp(scores - jnp.max(scores, axis=0, keepdims=True))
        probs = exponent * (1.0 / jnp.sum(exponent, axis=0, keepdims=True))
        value_grad = mm(probs.astype(BF16), mixed)
        prob_grad = mm_nt(value, mixed)
        held = probs * prob_grad
        score_grad = (held - probs * jnp.sum(held, axis=0, keepdims=True)).astype(BF16)
        grads[0].append(mm_tn(score_grad, key) * 0.125)
        grads[1].append(mm(score_grad, query))
        grads[2].append(value_grad)
    project_grad = jnp.concatenate(grads[0] + grads[1] + grads[2], axis=1).astype(BF16)
    grad = mm_nt(project_grad, weight_ref[...])
    sums_ref[0] = jnp.concatenate(
        [jnp.sum(grad, axis=0, keepdims=True), jnp.sum(grad * base, axis=0, keepdims=True)], axis=0
    )
    part_ref[0] = (middle_ref[0].astype(F32) + norm_pull(base, scale, grad * (1.0 + mod_ref[0, 1:2]))).astype(BF16)
    weight_grad = mm_tn(normed, project_grad)

    @pl.when(item == 0)
    def _():
        total_ref[...] = weight_grad

    @pl.when(item > 0)
    def _():
        total_ref[...] += weight_grad

    @pl.when(item == pl.num_programs(0) - 1)
    def _():
        if len(grad_refs) == 1:
            grad_refs[0][...] = total_ref[...].astype(BF16)
        else:
            store_blocks(*grad_refs, rank_ref[0], 0, total_ref[...].astype(BF16))


def attention_back(tokens, mod, weight, valid, projected, mixed, middle, rank, dp_size):
    items, length, width = tokens.shape
    columns = weight.shape[1]
    rows = width // dp_size
    each = pl.BlockSpec((1, length, width), lambda i: (i, 0, 0))
    if rows % 16:
        grads, blocks = (shaped(weight.shape, BF16),), (whole(weight.shape),)
    else:
        part = (dp_size // 2, 1, rows, columns)
        grads, blocks = (shaped(part, BF16),) * 2, (whole(part),) * 2
    result = call(
        functools.partial(attention_back_kernel, columns // (3 * HD)),
        (shaped(tokens.shape, BF16), shaped((items, 2, width), F32)) + grads,
        [
            pl.BlockSpec(memory_space=pltpu.SMEM),
            each,
            pl.BlockSpec((1, 6, width), lambda i: (i, 0, 0)),
            whole(weight.shape),
            pl.BlockSpec((1, length, 1), lambda i: (i, 0, 0)),
            pl.BlockSpec((1, length, columns), lambda i: (i, 0, 0)),
            pl.BlockSpec((1, 3 * length // 2, 128), lambda i: (i, 0, 0)),
            each,
        ],
        (each, pl.BlockSpec((1, 2, width), lambda i: (i, 0, 0))) + blocks,
        (rank, tokens, mod, weight, valid, projected, mixed, middle),
        grid=(items,),
        scratch=[pltpu.VMEM(weight.shape, F32)],
        flops=10_000_000_000,
        moved=12_000_000,
        name="attention_back",
    )
    if rows % 16:
        result = tuple(result[:2]) + split_blocks(result[2][None], dp_size)
    return result


def body(
    tokens,
    time_embed,
    class_embed,
    valid_mask,
    routes,
    gate_logits,
    ada_weight,
    ada_bias,
    qkv_weight,
    out_weight,
    out_bias,
    fc1_weight,
    fc1_bias,
    fc2_weight,
    fc2_bias,
    expert_in,
    expert_out,
    out_grad,
):
    items, local, width = tokens.shape
    ranks = lax.axis_size("tensor")
    rank = lax.axis_index("tensor")
    dp_size = lax.axis_size("dp")
    dp_rank = lax.axis_index("dp")
    length = local * ranks
    head_width = qkv_weight.shape[2]
    cols = ada_weight.shape[2]
    rows = width // dp_size
    start = rank * local
    bits = dp_size.bit_length() - 1
    forth = list(range(bits))
    back = [0] + list(range(bits - 1, 0, -1))
    dp_index = dp_rank.astype(I32).reshape(1)

    def own_rows(values):
        return lax.dynamic_slice_in_dim(values, start, local, 1)

    tokens_full = lax.all_gather(tokens, "tensor", axis=1, tiled=True)
    out_turned = out_weight.T
    share_rows = head_width // dp_size
    piece = lax.dynamic_slice_in_dim(out_turned, dp_rank * share_rows, share_rows, 0)
    pieces = jnp.concatenate(gather_parts(piece), axis=0)
    condition = time_embed + class_embed
    cond_wide, silu_pull = jax.vjp(jax.nn.silu, condition)
    cond_low = cond_wide.astype(BF16)
    bias_cols = lax.dynamic_slice_in_dim(ada_bias, rank * cols, cols, 1)
    modulation_local = dot("id,dsk->isk", cond_low, ada_weight) + bias_cols.astype(F32)[None]
    modulation = jnp.concatenate(gather_parts(modulation_local), axis=2)
    modulation = swing(modulation, width - rank * cols, 2)

    first = after(expert_in, modulation).transpose(1, 0, 2)
    second = after(expert_out, modulation).transpose(1, 0, 2)
    qkv = qkv_weight.reshape(width, 3 * head_width)
    chosen = routes.transpose(0, 2, 1)
    live = valid_mask[:, None, :] > 0
    expert_ids = jnp.arange(E, dtype=I32)
    named = (chosen[:, :, None, :] == expert_ids[None, None, :, None]) & live[:, :, None, :]
    choose = jnp.any(named, axis=1)
    place = jnp.arange(length, dtype=I32)
    earlier = (place[:, None] < place[None, :]).astype(BF16)
    before = dot("iet,ts->ies", choose.astype(BF16), earlier).astype(I32)
    position = jnp.sum(jnp.where(named, before[:, None], 0), axis=2)
    marks = jnp.where(live, chosen * CAP + position, -1)
    columns = marks.transpose(0, 2, 1)
    gate_soft = jax.nn.softmax(gate_logits, axis=-1)
    share = gate_soft.transpose(0, 2, 1) * live

    every = dp_gather(jnp.concatenate([pieces, cond_low], axis=0))
    cond_every = every[:, ranks * share_rows :]
    out_full = every[:, : ranks * share_rows].reshape(dp_size, ranks, share_rows, width)
    out_full = out_full.swapaxes(0, 1).reshape(ranks, head_width, width)
    out_full = swing(out_full, ranks - rank, 0)
    modulation = after(modulation, first, second, marks, columns, share)
    projected, mixed = attention(tokens_full, modulation, qkv, valid_mask[:, None, :])
    mixed_full = lax.all_gather(mixed, "tensor", axis=0)
    grad_full = lax.all_gather(after(out_grad, mixed_full), "tensor", axis=1, tiled=True)

    middle, branch_attn, normed_mlp = middle_part(
        mixed_full, out_full, out_bias[None], tokens_full, modulation
    )
    buffer, expert_act, expert_slope, hidden_act, hidden_slope, mlp_part = forward_part(
        normed_mlp, marks, share, columns, fc1_weight, fc1_bias[None], fc2_weight, first, second
    )
    mlp_sum = lax.psum_scatter(mlp_part, "tensor", scatter_dimension=1, tiled=True)

    quick = rows % 16 == 0 and dp_size == 8
    halfway = E // 2

    def start_sum(keep, send):
        return keep, dp_exchange(send, 0)

    def second_step(pair, order):
        keep, other = pair
        if not quick:
            return keep, other
        kept, sent = halve(keep, other, 0 if order[0] == 2 else 1)
        return kept, sent

    def third_step(pair, order):
        if not quick:
            return pair
        kept, sent = pair
        return halve(kept, dp_exchange(sent, order[0]), 0)

    def final_step(pair, order):
        if not quick:
            keep, other = pair
            return dp_scatter((keep.astype(F32) + other.astype(F32)).astype(BF16), order, BF16)
        kept, sent = pair
        return kept[0], dp_exchange(sent, order[1])[0]

    def whole_sum(pairs):
        if quick:
            return last(pairs, halfway)
        experts = jnp.concatenate([pair[:halfway] for pair in pairs], axis=0).swapaxes(0, 1).astype(F32)
        return [experts] + [pair[halfway].astype(F32) for pair in pairs if pair.shape[0] > halfway]

    ahead, behind = forth[1:], back[1:]
    branch_grad, branch_slot, keep, send = slots_part(
        0, halfway, marks, expert_act, dp_index, dp_size, grad=grad_full, mod=modulation, hidden=hidden_act
    )
    out_low = start_sum(keep, send)
    branch_slot, keep, send = slots_part(
        halfway, E - halfway, marks, expert_act, dp_index, dp_size, branch=branch_grad, held=branch_slot
    )
    out_high = start_sum(keep, send)
    out_low = second_step(out_low, ahead)
    out_high = second_step(out_high, behind)
    up_grad, hidden_grad, fc1_bias_part, normed_mlp_grad, gate_part = back_part(
        branch_grad,
        after(columns, out_low[1], out_high[1]),
        fc1_weight,
        fc2_weight,
        hidden_slope,
        branch_slot,
        expert_act,
        expert_slope,
        first,
        second,
    )
    out_low = third_step(out_low, ahead)
    out_high = third_step(out_high, behind)
    own = jnp.stack([start, start + local]).astype(I32)
    middle_grad, low_grad, mixed_parts, sums = second_norm_part(
        normed_mlp_grad,
        middle,
        branch_attn,
        grad_full,
        mlp_part,
        after(modulation, out_low[1], out_high[1]),
        out_full,
        own,
    )
    mixed_grad = lax.psum_scatter(mixed_parts, "tensor", scatter_dimension=0)

    marker = after(dp_index, mixed_parts)
    in_low = start_sum(
        *first_part(0, halfway, buffer, up_grad, (normed_mlp, hidden_grad), False, marker, dp_size)
    )
    in_high = start_sum(
        *first_part(halfway, E - halfway, buffer, up_grad, (low_grad, mixed_full), True, marker, dp_size)
    )
    out_low = final_step(out_low, ahead)
    out_high = final_step(out_high, behind)
    in_low = second_step(in_low, ahead)
    in_high = second_step(in_high, behind)

    gate = after(modulation, in_low[1], in_high[1], out_low, out_high)
    tokens_part, attn_sums, qkv_keep, qkv_send = attention_back(
        tokens_full, gate, qkv, valid_mask[:, :, None], projected, mixed_grad, middle_grad, dp_index, dp_size
    )
    tokens_grad = lax.psum_scatter(tokens_part, "tensor", scatter_dimension=1, tiled=True)
    qkv_other = dp_exchange(qkv_send, 0)

    sums, mlp_sum, branch_grad, gate_part, fc1_bias_part, out_low, out_high = lax.optimization_barrier(
        (sums, mlp_sum, branch_grad, gate_part, fc1_bias_part, out_low, out_high, tokens_part)
    )[:7]
    gate_mlp_grad = sums[:, 4] + jnp.sum(out_grad.astype(F32) * fc2_bias.astype(F32), axis=1)
    branch_mlp = mlp_sum.astype(F32) + fc2_bias.astype(F32)
    output = (own_rows(middle) + modulation[:, 5][:, None] * branch_mlp).astype(BF16)
    expert_out_sum, fc2_sum = whole_sum([out_low, out_high])

    def finish(keep, other, order):
        total = keep.astype(F32) + other.astype(F32)
        return dp_scatter(total.astype(BF16), order, BF16)

    in_low = third_step(in_low, ahead)
    in_high = third_step(in_high, behind)
    expert_in_sum, fc1_sum, out_sum = whole_sum([final_step(in_low, ahead), final_step(in_high, behind)])
    out_sum = swing(out_sum, rank * head_width, 1)
    out_sum = scatter_sum(
        [out_sum[:, step * head_width : (step + 1) * head_width] for step in range(ranks)]
    )
    qkv_sum = finish(qkv_keep, qkv_other, ahead)[0]
    qkv_sum = qkv_sum.astype(F32).reshape(rows, 3, head_width)

    fine = rows // ranks
    gate_part = gate_part[..., 0] + gate_part[..., 1]
    gate_turn = swing(gate_part, start, 2).reshape(items, 2, ranks, local)
    gate_turn = gate_turn.transpose(2, 0, 1, 3).reshape(ranks, -1)
    fc2_bias_part = jnp.sum(own_rows(branch_grad).astype(F32), axis=(0, 1))
    bias_parts = jnp.stack([fc2_bias_part, jnp.sum(sums[:, 3], axis=0)])
    bias_turn = bias_parts.reshape(2, dp_size, ranks, fine).transpose(2, 0, 1, 3).reshape(ranks, -1)
    bias_turn = swing(bias_turn, rank, 0)
    small = jnp.concatenate([gate_turn, bias_turn], axis=1)
    small = scatter_sum([small[step] for step in range(ranks)])
    gate_grad = small[: items * 2 * local].reshape(items, 2, local).transpose(0, 2, 1)
    bias_own = small[items * 2 * local :].reshape(2, dp_size, fine)
    gate_logits_grad = gate_grad - own_rows(gate_soft) * jnp.sum(gate_grad, axis=-1, keepdims=True)
    bias_blocks = jnp.concatenate(
        [bias_own[0], bias_own[1], fc1_bias_part.reshape(dp_size, rows)], axis=1
    )
    bias_sum = dp_scatter(to_relative(bias_blocks), forth, F32)

    modulation_part = jnp.stack(
        [attn_sums[:, 0], attn_sums[:, 1], sums[:, 2], sums[:, 0], sums[:, 1], gate_mlp_grad],
        axis=1,
    )
    modulation_part = swing(modulation_part, rank * cols, 2)
    modulation_grad = scatter_sum(
        [modulation_part[:, :, step * cols : (step + 1) * cols] for step in range(ranks)]
    ).astype(BF16)
    cond_act_grad = dot("isk,dsk->id", modulation_grad, ada_weight)
    condition_part = silu_pull(cond_act_grad)[0]
    condition_part = swing(condition_part, rank * cols, 1)
    condition_grad = scatter_sum(
        [condition_part[:, step * cols : (step + 1) * cols] for step in range(ranks)]
    )
    modulation_every = dp_gather(modulation_grad)
    cond_every = cond_every.reshape(dp_size * items, width)
    cond_rows = lax.dynamic_slice_in_dim(cond_every, dp_rank * rows, rows, 1)
    modulation_every = modulation_every.reshape(dp_size * items, 6, cols)
    ada_weight_sum = dot("id,isk->dsk", cond_rows, modulation_every)
    ada_bias_sum = jnp.sum(modulation_every.astype(F32), axis=0)
    ada_bias_sum = lax.dynamic_slice_in_dim(
        ada_bias_sum, dp_rank * (cols // dp_size), cols // dp_size, 1
    )
    return (
        output,
        tokens_grad,
        condition_grad,
        gate_logits_grad,
        ada_weight_sum,
        ada_bias_sum,
        qkv_sum,
        out_sum,
        bias_sum[fine : 2 * fine],
        fc1_sum,
        bias_sum[2 * fine :],
        fc2_sum,
        bias_sum[:fine],
        expert_in_sum,
        expert_out_sum,
    )


def solution(mesh):
    in_specs = (
        P("dp", "tensor", None),
        P("dp", None),
        P("dp", None),
        P("dp", None),
        P("dp", None, None),
        P("dp", None, None),
        P(None, None, "tensor"),
        P(),
        P(None, None, "tensor"),
        P(None, "tensor"),
        P(),
        P(None, "tensor"),
        P("tensor"),
        P(None, "tensor"),
        P(),
        P(None, None, "tensor"),
        P(None, None, "tensor"),
        P("dp", "tensor", None),
    )
    out_specs = (
        P("dp", "tensor", None),
        P("dp", "tensor", None),
        P("dp", "tensor"),
        P("dp", "tensor", None),
        P("dp", None, "tensor"),
        P(None, ("tensor", "dp")),
        P("dp", None, "tensor"),
        P("dp", "tensor"),
        P(("dp", "tensor")),
        P("dp", "tensor"),
        P(("tensor", "dp")),
        P("dp", "tensor"),
        P(("dp", "tensor")),
        P("dp", None, "tensor"),
        P("dp", None, "tensor"),
    )
    return jax.shard_map(body, mesh=mesh, in_specs=in_specs, out_specs=out_specs, check_vma=False)
```

time: 1070 us -> 414 us (0.39)
  waiting for transfers between devices: 642 us -> 110 us
  matrix products: 201 us -> 2.29 us
  Pallas kernels: 0 us -> 177 us
  local copies, waits for them, and re-layouts: 98.5 us -> 35.4 us
  blocking collectives: 52.4 us -> 0 us
  starting transfers between devices: 2.04 us -> 45.5 us
  other arithmetic: 49.6 us -> 20.6 us
    reduce_scatter x11 -> x3, waiting for transfers between devices: 551 us -> 15.9 us  [the longest x1 15.9 us: body(): lax.psum_scatter(mlp_part, 'tensor', scatter_dimension=1, tiled=True)]
    dot_general x38 -> x4, matrix products: 201 us -> 2.29 us  [dot(): return jnp.einsum(spec, left, right, preferred_element_type=F32)]
    pallas_call x0 -> x20, Pallas kernels: none -> 177 us  [call(): pl.pallas_call(kernel, out_shape=out_shape, grid=grid, in_specs=in_specs,...]
    ppermute x0 -> x42, waiting for transfers between devices: none -> 68.9 us  [the longest x24 60.2 us: dp_exchange(): return lax.ppermute(values, 'dp', [(i, i ^ 1 << bit) for i in range(size)])]
    all_gather x4 -> x3, waiting for transfers between devices: 88.8 us -> 25.5 us  [the longest x1 22.2 us: body(): mixed_full = lax.all_gather(mixed, 'tensor', axis=0)]
    ppermute x0 -> x42, starting transfers between devices: none -> 45.3 us  [the longest x24 18.8 us: dp_exchange(): return lax.ppermute(values, 'dp', [(i, i ^ 1 << bit) for i in range(size)])]
    transpose x5 -> x2, local copies, waits for them, and re-layouts: 52.2 us -> 17.7 us  [the longest x1 17.7 us: body(): second = after(expert_out, modulation).transpose(1, 0, 2)]
    unnamed x2 -> x0, blocking collectives: 31.2 us -> none
  transfers between devices with their start and end apart: 19 -> 48, of which waited for: 14 -> 19; matrix products, arithmetic and copies ran while one was open for 19% -> 11% of each run, Pallas kernels for 0% -> 35%
where the time goes in v1:
time: 414 us; the launch traced here: 406 us
  Pallas kernels  177 us (43%)
  waiting for transfers between devices  110 us (27%)
  starting transfers between devices  45.5 us (11%)
  local copies, waits for them, and re-layouts  35.4 us (9%)
  other arithmetic  20.6 us (5%)
  between operations  15 us (4%)
    pallas_call x20, Pallas kernels, call(): pl.pallas_call(kernel, out_shape=out_shape, grid=grid, in_specs=in_specs,...  177 us
    ppermute x24, waiting for transfers between devices, dp_exchange(): return lax.ppermute(values, 'dp', [(i, i ^ 1 << bit) for i in range(size)])  60.2 us
    all_gather x1, waiting for transfers between devices, body(): mixed_full = lax.all_gather(mixed, 'tensor', axis=0)  22.2 us
    ppermute x24, starting transfers between devices, dp_exchange(): return lax.ppermute(values, 'dp', [(i, i ^ 1 << bit) for i in range(size)])  18.8 us
    transpose x1, local copies, waits for them, and re-layouts, body(): second = after(expert_out, modulation).transpose(1, 0, 2)  17.7 us
    reduce_scatter x1, waiting for transfers between devices, body(): lax.psum_scatter(mlp_part, 'tensor', scatter_dimension=1, tiled=True)  15.9 us
    ppermute x12, starting transfers between devices, to_rank(): lax.ppermute(values, 'tensor', [(i, (i + step) % size) for i in range(siz...  15.7 us
    ppermute x6, starting transfers between devices, from_rank(): lax.ppermute(values, 'tensor', [(i, (i - step) % size) for i in range(siz...  10.8 us
  transfers between devices with their start and end apart: 48, of which 19 were waited for; matrix products, arithmetic and copies ran while one was open for 11% of the time, Pallas kernels for 35%

profile of v1, /device:TPU:0, one launch (start us, length us, event | category | flops | bytes accessed | tf_op | source)
XLA Modules:
  0.0 406.4 jit_solution(2550035771152707278)
XLA Ops:
  31.2 17.7 %copy_bitcast_fusion = (bf16[8,768,768]{2,1,0:T(8,128)(2,1)}, bf16[8,768,768]{2,1,0:T(8,128)(2,1)}) fusion(bf16[768,8,768]{2,1,0:T(8,128)(2,1)} %param.34, bf16[768,8,768]{2,1,0:T(8,128)(2,1)} %param.33), kind=kLoop, calls=%fused_computation.2 | loop fusion | bytes 37748736 | tf_op jit(solution)/shard_map/transpose | solution.py:928
  52.1 7.5 %attention_forward.1 = (bf16[2,512,576]{2,1,0:T(8,128)(2,1)}, bf16[2,768,128]{2,1,0:T(8,128)(2,1)}) custom-call(bf16[2,512,768]{2,1,0:T(8,128)(2,1)} %all-gather.5.cloned.1.call-done.tokens_ref, f32[2,6,768]{2,1,0:T(8,128)} %constant_dynamic-slice_fusion.3.mod_ref.refs_1_, bf16[768,576]{1,0:T(8,128)(2,1)} %copy.169.weight_ref, ...), custom_call_target="tpu_custom_call" | custom-call | flops 8000000000 | bytes 6000000 | tf_op jit(solution)/shard_map/attention_forward/pallas_call | solution.py:132
  62.7 8.1 %collective-permute-done.7 = bf16[2,98,768]{2,1,0:T(8,128)(2,1)S(1)} collective-permute-done((bf16[2,98,768]{2,1,0:T(8,128)(2,1)S(1)}, bf16[2,98,768]{2,1,0:T(8,128)(2,1)S(1)}, u32[]{:S(2)}, u32[]{:S(2)}) %collective-permute-start.7) | collective-permute-done | bytes 301088 | tf_op jit(solution)/shard_map/ppermute | solution.py:68
  73.5 22.2 %all-gather.9.cloned.1.call-done = bf16[8,768,128]{2,1,0:T(8,128)(2,1)} async-done(((bf16[2,768,128]{2,1,0:T(8,128)(2,1)}), bf16[8,768,128]{2,1,0:T(8,128)(2,1)}) %all-gather.9.cloned.1.call-update) | async-done | bytes 1572880 | tf_op jit(solution)/shard_map/all_gather | solution.py:951
  99.9 6.9 %middle.1 = (f32[2,512,768]{2,1,0:T(8,128)}, bf16[2,512,768]{2,1,0:T(8,128)(2,1)}, bf16[2,512,768]{2,1,0:T(8,128)(2,1)}) custom-call(bf16[4,2,768,128]{3,2,1,0:T(8,128)(2,1)} %bitcast.159, bf16[4,2,768,128]{3,2,1,0:T(8,128)(2,1)} %bitcast.160, bf16[4,192,768]{2,1,0:T(8,128)(2,1)} %fusion.3.weight_ref, bf16[1,768]{1,0:T(2,128)(2,1)} %broadcast_in_dim.67.bias_ref, ...), custom_call_target="tpu_custom_call" | custom-call | flops 3000000000 | bytes 12000000 | tf_op jit(solution)/shard_map/middle/pallas_call | solution.py:132
  106.8 30.4 %mlp_forward.1 = (bf16[8,384,768]{2,1,0:T(8,128)(2,1)}, bf16[8,384,768]{2,1,0:T(8,128)(2,1)}, bf16[8,384,768]{2,1,0:T(8,128)(2,1)}, bf16[2,512,768]{2,1,0:T(8,12...) custom-call(bf16[2,512,768]{2,1,0:T(8,128)(2,1)} %get-tuple-element.93.normed_ref.dense_left_ref, ...), custom_call_target="tpu_custom_call" | custom-call | flops 14000000000 | bytes 40000000 | tf_op jit(solution)/shard_map/mlp_forward/pallas_call | solution.py:132
  137.3 11.4 %weight_grads.4 = (bf16[2,512,768]{2,1,0:T(8,128)(2,1)}, bf16[8,384,768]{2,1,0:T(8,128)(2,1)}, bf16[4,5,96,768]{3,2,1,0:T(8,128)(2,1)}, bf16[4,5,96,768]{3,2,1,0:T(8,128)(2,1)}) custom-call(s32[1]{0:T(128)} %bitcast.14.rank_ref, s32[2,2,512]{2,1,0:T(2,128)} %add_select_fusion.marks_ref, bf16[8,384,768]{2,1,0:T(8,128)(2,1)} %get-tuple-element.94.act_ref, ...), custom_call_target="tpu_custom_call" | custom-call | flops 5000000000 | bytes 20000000 | tf_op jit(solution)/shard_map/weight_grads/pallas_call | solution.py:132
  148.7 8.8 %weight_grads.5 = (bf16[8,384,768]{2,1,0:T(8,128)(2,1)}, bf16[4,4,96,768]{3,2,1,0:T(8,128)(2,1)}, bf16[4,4,96,768]{3,2,1,0:T(8,128)(2,1)}) custom-call(s32[1]{0:T(128)} %bitcast.14.rank_ref, s32[2,2,512]{2,1,0:T(2,128)} %add_select_fusion.marks_ref, bf16[8,384,768]{2,1,0:T(8,128)(2,1)} %get-tuple-element.94.act_ref, ...), custom_call_target="tpu_custom_call", output_to_operand_aliasing={{0}: (4, {})} | custom-call | flops 5000000000 | bytes 20000000 | tf_op jit(solution)/shard_map/weight_grads/pallas_call | solution.py:132
  159.6 4.1 %halve.8 = (bf16[2,1,5,96,768]{4,3,2,1,0:T(8,128)(2,1)}, bf16[2,1,5,96,768]{4,3,2,1,0:T(8,128)(2,1)}) custom-call(bf16[2,2,5,96,768]{4,3,2,1,0:T(8,128)(2,1)} %bitcast.129, bf16[2,2,5,96,768]{4,3,2,1,0:T(8,128)(2,1)} %bitcast.130), custom_call_target="tpu_custom_call" | custom-call | flops 2949120 | bytes 8847360 | tf_op jit(solution)/shard_map/halve/pallas_call | solution.py:132
  165.2 3.6 halve.9
  170.8 28.9 %mlp_back.1 = (bf16[8,384,768]{2,1,0:T(8,128)(2,1)}, bf16[2,512,768]{2,1,0:T(8,128)(2,1)}, f32[1,768]{1,0:T(1,128)}, f32[2,512,768]{2,1,0:T(8,128)}, f32[2,2,512,128]{3,2,1,0:T(8,128)}) custom-call(bf16[2,512,768]{2,1,0:T(8,128)(2,1)} %get-tuple-element.142.refs_0_.branch_ref, s32[2,512,2]{2,1,0:T(8,128)} %fusion.11.columns_ref, bf16[768,768]{1,0:T(8,128)(2,1)} %fc1_ref.3, ...), custom_call_target="tpu_custom_call" | custom-call | flops 12000000000 | bytes 40000000 | tf_op jit(solution)/shard_map/mlp_back/pallas_call | solution.py:132
  206.8 13.4 %second_norm_back.1 = (bf16[2,512,768]{2,1,0:T(8,128)(2,1)}, bf16[2,512,768]{2,1,0:T(8,128)(2,1)}, bf16[4,2,768,128]{3,2,1,0:T(8,128)(2,1)}, f32[2,5,768]{2,1,0:T(8,128)}) custom-call(f32[2,512,768]{2,1,0:T(8,128)} %get-tuple-element.109.grad_ref, f32[2,512,768]{2,1,0:T(8,128)} %get-tuple-element.92.middle_ref, ...), custom_call_target="tpu_custom_call" | custom-call | flops 3000000000 | bytes 15000000 | tf_op jit(solution)/shard_map/second_norm_back/pallas_call | solution.py:132
  220.3 9.8 %weight_grads.7 = (bf16[4,5,96,768]{3,2,1,0:T(8,128)(2,1)}, bf16[4,5,96,768]{3,2,1,0:T(8,128)(2,1)}) custom-call(s32[1]{0:T(128)} %bitcast.14.rank_ref, bf16[8,384,768]{2,1,0:T(8,128)(2,1)} %get-tuple-element.124.left_ref, bf16[8,384,768]{2,1,0:T(8,128)(2,1)} %get-tuple-element.125.right_ref, bf16[2,512,768]{2,1,0:T(8,128)(2,1)} %get-tuple-element.130.dense_left_ref, ...), custom_call_target="tpu_custom_call" | custom-call | flops 5000000000 | bytes 20000000 | tf_op jit(solution)/shard_map/weight_grads/pallas_call | solution.py:132
  230.1 9.6 %weight_grads.6 = (bf16[4,5,96,768]{3,2,1,0:T(8,128)(2,1)}, bf16[4,5,96,768]{3,2,1,0:T(8,128)(2,1)}) custom-call(s32[1]{0:T(128)} %bitcast.14.rank_ref, bf16[8,384,768]{2,1,0:T(8,128)(2,1)} %get-tuple-element.124.left_ref, bf16[8,384,768]{2,1,0:T(8,128)(2,1)} %get-tuple-element.125.right_ref, ...), custom_call_target="tpu_custom_call" | custom-call | flops 5000000000 | bytes 20000000 | tf_op jit(solution)/shard_map/weight_grads/pallas_call | solution.py:132
  243.3 4.1 %halve.13 = (bf16[1,2,5,96,768]{4,3,2,1,0:T(8,128)(2,1)}, bf16[1,2,5,96,768]{4,3,2,1,0:T(8,128)(2,1)}) custom-call(bf16[2,2,5,96,768]{4,3,2,1,0:T(8,128)(2,1)} %bitcast.128, bf16[2,2,5,96,768]{4,3,2,1,0:T(8,128)(2,1)} %bitcast.36.other_ref), custom_call_target="tpu_custom_call" | custom-call | flops 2949120 | bytes 8847360 | tf_op jit(solution)/shard_map/halve/pallas_call | solution.py:132
  247.5 4.2 %halve.12 = (bf16[2,1,5,96,768]{4,3,2,1,0:T(8,128)(2,1)}, bf16[2,1,5,96,768]{4,3,2,1,0:T(8,128)(2,1)}) custom-call(bf16[2,2,5,96,768]{4,3,2,1,0:T(8,128)(2,1)} %bitcast.127, bf16[2,2,5,96,768]{4,3,2,1,0:T(8,128)(2,1)} %bitcast.33.other_ref), custom_call_target="tpu_custom_call" | custom-call | flops 2949120 | bytes 8847360 | tf_op jit(solution)/shard_map/halve/pallas_call | solution.py:132
  251.6 4.5 %collective-permute-done.14 = bf16[1,4,96,768]{3,2,1,0:T(8,128)(2,1)} collective-permute-done((bf16[1,4,96,768]{3,2,1,0:T(8,128)(2,1)}, bf16[1,4,96,768]{3,2,1,0:T(8,128)(2,1)}, u32[]{:S(2)}, u32[]{:S(2)}) %collective-permute-start.14) | collective-permute-done | bytes 589856 | tf_op jit(solution)/shard_map/ppermute | solution.py:68
  259.1 14.2 %attention_back.1 = (bf16[2,512,768]{2,1,0:T(8,128)(2,1)}, f32[2,2,768]{2,1,0:T(2,128)}, bf16[4,1,96,576]{3,2,1,0:T(8,128)(2,1)}, bf16[4,1,96,576]{3,2,1,0:T(8,128)(2,1)}) custom-call(s32[1]{0:T(128)} %bitcast.14.rank_ref, bf16[2,512,768]{2,1,0:T(8,128)(2,1)} %all-gather.5.cloned.1.call-done.tokens_ref, ...), custom_call_target="tpu_custom_call" | custom-call | flops 10000000000 | bytes 12000000 | tf_op jit(solution)/shard_map/attention_back/pallas_call | solution.py:132
  273.3 15.9 %reduce-scatter.4.cloned.1.call-done = bf16[2,128,768]{2,1,0:T(8,128)(2,1)} async-done(((bf16[2,512,768]{2,1,0:T(8,128)(2,1)}), bf16[2,128,768]{2,1,0:T(8,128)(2,1)}) %reduce-scatter.4.cloned.1.call-update) | async-done | bytes 393232 | tf_op jit(solution)/shard_map/reduce_scatter | solution.py:960
  295.6 3.4 collective-permute-start.25
  308.5 4.0 last_sum.3
  312.5 21.4 %collective-permute-done.40 = f32[2,144]{1,0:T(2,128)S(1)} collective-permute-done((f32[2,144]{1,0:T(2,128)S(1)}, f32[2,144]{1,0:T(2,128)S(1)}, u32[]{:S(2)}, u32[]{:S(2)}) %collective-permute-start.40) | collective-permute-done | bytes 1184 | tf_op jit(solution)/shard_map/ppermute | solution.py:68
  367.5 15.1 %collective-permute-done.30 = bf16[2,1,96,576]{2,3,1,0:T(8,128)(2,1)S(1)} collective-permute-done((bf16[2,1,96,576]{2,3,1,0:T(8,128)(2,1)}, bf16[2,1,96,576]{2,3,1,0:T(8,128)(2,1)S(1)}, u32[]{:S(2)}, u32[]{:S(2)}) %collective-permute-start.30) | collective-permute-done | bytes 221216 | tf_op jit(solution)/shard_map/ppermute | solution.py:68
  384.2 4.1 %last_sum.2 = (f32[96,8,768]{2,1,0:T(8,128)}, f32[96,768]{1,0:T(8,128)}, f32[96,768]{1,0:T(8,128)}) custom-call(bf16[5,96,768]{2,1,0:T(8,128)(2,1)} %bitcast.140, bf16[5,96,768]{2,1,0:T(8,128)(2,1)} %bitcast.141, bf16[5,96,768]{2,1,0:T(8,128)(2,1)} %bitcast.139, bf16[5,96,768]{2,1,0:T(8,128)(2,1)} %bitcast.64.refs_3_), custom_call_target="tpu_custom_call" | custom-call | flops 737280 | bytes 5898240 | tf_op jit(solution)/shard_map/last_sum/pallas_call | solution.py:132
  (244 shorter events, 117.9 us)
Async XLA Ops:
  7.2 44.9 %all-gather.5.cloned.1.call-start = ((), (), s32[]{:S(2)}) async-start(), calls=%async_computation.3 | async-start | bytes 1966080 | tf_op jit(solution)/shard_map/all_gather | solution.py:914
  8.1 14.6 %collective-permute-start.5 = (bf16[24,768]{1,0:T(8,128)(2,1)S(1)}, bf16[24,768]{1,0:T(8,128)(2,1)S(1)}, u32[]{:S(2)}, u32[]{:S(2)}) collective-permute-start(bf16[24,768]{1,0:T(8,128)(2,1)S(1)} %get-tuple-element.258), channel_id=1, source_target_pairs={{0,1},{1,2},{2,3},{3,0},{4,5},{5,6},{6,7},{7,4},{8,9},{9,10},{10,1... | collective-permute-start | bytes 110600 | tf_op jit(solution)/shard_map/ppermute | solution.py:41
  11.2 11.5 %collective-permute-start.4 = (bf16[24,768]{1,0:T(8,128)(2,1)S(1)}, bf16[24,768]{1,0:T(8,128)(2,1)S(1)}, u32[]{:S(2)}, u32[]{:S(2)}) collective-permute-start(bf16[24,768]{1,0:T(8,128)(2,1)S(1)} %get-tuple-element.258), channel_id=1, source_target_pairs={{0,2},{1,3},{2,0},{3,1},{4,6},{5,7},{6,4},{7,5},{8,10},{9,11},{10,... | collective-permute-start | bytes 110600 | tf_op jit(solution)/shard_map/ppermute | solution.py:41
  15.1 80.6 %all-gather.9.cloned.1.call-start = ((), (), s32[]{:S(2)}) async-start(), calls=%async_computation.8 | async-start | bytes 1966080 | tf_op jit(solution)/shard_map/all_gather | solution.py:951
  59.7 77.6 %all-gather.7.cloned.1.call-start = ((), (), s32[]{:S(2)}) async-start(), calls=%async_computation.4 | async-start | bytes 1966080 | tf_op jit(solution)/shard_map/all_gather | solution.py:952
  61.2 9.6 %collective-permute-start.7 = (bf16[2,98,768]{2,1,0:T(8,128)(2,1)S(1)}, bf16[2,98,768]{2,1,0:T(8,128)(2,1)S(1)}, u32[]{:S(2)}, u32[]{:S(2)}) collective-permute-start(bf16[2,98,768]{2,1,0:T(8,128)(2,1)S(1)} %pad_maximum_fusion.1), channel_id=1, source_target_pairs={{0,8},{4,12},{8,0},{12,4},{16,24},{20,28},{24,16},{28,20},{1,9},{5... | collective-permute-start | bytes 903176 | tf_op jit(solution)/shard_map/ppermute | solution.py:68
  72.0 25.0 %collective-permute-start.8 = (bf16[4,98,768]{2,0,1:T(4,128)(2,1)S(1)}, bf16[4,98,768]{2,0,1:T(4,128)(2,1)}, u32[]{:S(2)}, u32[]{:S(2)}) collective-permute-start(bf16[4,98,768]{2,0,1:T(4,128)(2,1)S(1)} %copy.170), channel_id=1, source_target_pairs={{0,16},{4,20},{8,24},{12,28},{16,0},{20,4},{24,8},{28,12},{1,17},{... | collective-permute-start | bytes 1806344 | tf_op jit(solution)/shard_map/ppermute | solution.py:68
  95.7 163.4 %reduce-scatter.6.cloned.1.call-start = ((), (), s32[]{:S(2)}) async-start(), calls=%async_computation.6 | async-start | bytes 1966080 | tf_op jit(solution)/shard_map/reduce_scatter | solution.py:1030
  163.7 39.8 %collective-permute-start.11 = (bf16[2,5,96,768]{3,2,1,0:T(8,128)(2,1)}, bf16[2,5,96,768]{3,2,1,0:T(8,128)(2,1)}, u32[]{:S(2)}, u32[]{:S(2)}) collective-permute-start(bf16[2,5,96,768]{3,2,1,0:T(8,128)(2,1)} %bitcast.164), channel_id=1, source_target_pairs={{0,8},{4,12},{8,0},{12,4},{16,24},{20,28},{24,16},{28,20},{1,9},{5... | collective-permute-start | bytes 4423688 | tf_op jit(solution)/shard_map/ppermute | solution.py:68
  168.8 30.9 %collective-permute-start.12 = (bf16[2,4,96,768]{3,2,1,0:T(8,128)(2,1)}, bf16[2,4,96,768]{3,2,1,0:T(8,128)(2,1)S(1)}, u32[]{:S(2)}, u32[]{:S(2)}) collective-permute-start(bf16[2,4,96,768]{3,2,1,0:T(8,128)(2,1)} %bitcast.165), channel_id=1, source_target_pairs={{0,16},{4,20},{8,24},{12,28},{16,0},{20,4},{24,8},{28,12},{1,17},{... | collective-permute-start | bytes 3538952 | tf_op jit(solution)/shard_map/ppermute | solution.py:68
  220.3 68.9 %reduce-scatter.4.cloned.1.call-start = ((), (), s32[]{:S(2)}) async-start(), calls=%async_computation.5 | async-start | bytes 1966080 | tf_op jit(solution)/shard_map/reduce_scatter | solution.py:960
  230.1 13.2 %collective-permute-start.16 = (bf16[4,5,96,768]{3,2,1,0:T(8,128)(2,1)}, bf16[4,5,96,768]{3,2,1,0:T(8,128)(2,1)}, u32[]{:S(2)}, u32[]{:S(2)}) collective-permute-start(bf16[4,5,96,768]{3,2,1,0:T(8,128)(2,1)} %get-tuple-element.132), channel_id=1, source_target_pairs={{0,4},{4,0},{8,12},{12,8},{16,20},{20,16},{24,28},{28,24},{1,5},{5... | collective-permute-start | bytes 8847368 | tf_op jit(solution)/shard_map/ppermute | solution.py:68
  240.2 159.1 %reduce-scatter.8.cloned.1.call-start = ((), (), s32[]{:S(2)}) async-start(), calls=%async_computation.7 | async-start | bytes 1966080 | tf_op jit(solution)/shard_map/reduce_scatter | solution.py:1048
  240.3 18.8 %collective-permute-start.13 = (bf16[1,5,96,768]{3,2,1,0:T(8,128)(2,1)}, bf16[1,5,96,768]{3,2,1,0:T(8,128)(2,1)}, u32[]{:S(2)}, u32[]{:S(2)}) collective-permute-start(bf16[1,5,96,768]{3,2,1,0:T(8,128)(2,1)} %bitcast.166), channel_id=1, source_target_pairs={{0,16},{4,20},{8,24},{12,28},{16,0},{20,4},{24,8},{28,12},{1,17},{... | collective-permute-start | bytes 2211848 | tf_op jit(solution)/shard_map/ppermute | solution.py:68
  240.8 15.3 %collective-permute-start.14 = (bf16[1,4,96,768]{3,2,1,0:T(8,128)(2,1)}, bf16[1,4,96,768]{3,2,1,0:T(8,128)(2,1)}, u32[]{:S(2)}, u32[]{:S(2)}) collective-permute-start(bf16[1,4,96,768]{3,2,1,0:T(8,128)(2,1)} %bitcast.169), channel_id=1, source_target_pairs={{0,8},{4,12},{8,0},{12,4},{16,24},{20,28},{24,16},{28,20},{1,9},{5... | collective-permute-start | bytes 1769480 | tf_op jit(solution)/shard_map/ppermute | solution.py:68
  299.1 56.2 %collective-permute-start.34 = (bf16[2,5,96,768]{3,2,1,0:T(8,128)(2,1)}, bf16[2,5,96,768]{3,2,1,0:T(8,128)(2,1)}, u32[]{:S(2)}, u32[]{:S(2)}) collective-permute-start(bf16[2,5,96,768]{3,2,1,0:T(8,128)(2,1)} %bitcast.163), channel_id=1, source_target_pairs={{0,16},{4,20},{8,24},{12,28},{16,0},{20,4},{24,8},{28,12},{1,17},{... | collective-permute-start | bytes 4423688 | tf_op jit(solution)/shard_map/ppermute | solution.py:68
  300.6 58.4 %collective-permute-start.32 = (bf16[2,5,96,768]{3,2,1,0:T(8,128)(2,1)}, bf16[2,5,96,768]{3,2,1,0:T(8,128)(2,1)S(1)}, u32[]{:S(2)}, u32[]{:S(2)}) collective-permute-start(bf16[2,5,96,768]{3,2,1,0:T(8,128)(2,1)} %bitcast.162), channel_id=1, source_target_pairs={{0,8},{4,12},{8,0},{12,4},{16,24},{20,28},{24,16},{28,20},{1,9},{5... | collective-permute-start | bytes 4423688 | tf_op jit(solution)/shard_map/ppermute | solution.py:68
  305.5 28.5 %collective-permute-start.40 = (f32[2,144]{1,0:T(2,128)S(1)}, f32[2,144]{1,0:T(2,128)S(1)}, u32[]{:S(2)}, u32[]{:S(2)}) collective-permute-start(f32[2,144]{1,0:T(2,128)S(1)} %bitcast.156), channel_id=1, source_target_pairs={{0,8},{4,12},{8,0},{12,4},{16,24},{20,28},{24,16},{28,20},{1,9},{5... | collective-permute-start | bytes 3464 | tf_op jit(solution)/shard_map/ppermute | solution.py:68
  307.1 32.3 %collective-permute-start.17 = (f32[2,6,192]{2,1,0:T(8,128)S(1)}, f32[2,6,192]{2,1,0:T(8,128)S(1)}, u32[]{:S(2)}, u32[]{:S(2)}) collective-permute-start(f32[2,6,192]{2,1,0:T(8,128)S(1)} %get-tuple-element.277), channel_id=1, source_target_pairs={{0,1},{1,2},{2,3},{3,0},{4,5},{5,6},{6,7},{7,4},{8,9},{9,10},{10,1... | collective-permute-start | bytes 27656 | tf_op jit(solution)/shard_map/ppermute | solution.py:46
  307.1 32.3 %collective-permute-start.18 = (f32[2,6,192]{2,1,0:T(8,128)S(1)}, f32[2,6,192]{2,1,0:T(8,128)S(1)}, u32[]{:S(2)}, u32[]{:S(2)}) collective-permute-start(f32[2,6,192]{2,1,0:T(8,128)S(1)} %get-tuple-element.278), channel_id=1, source_target_pairs={{0,2},{1,3},{2,0},{3,1},{4,6},{5,7},{6,4},{7,5},{8,10},{9,11},{10,... | collective-permute-start | bytes 27656 | tf_op jit(solution)/shard_map/ppermute | solution.py:46
  358.4 24.9 %collective-permute-start.35 = (bf16[1,5,96,768]{3,2,1,0:T(8,128)(2,1)}, bf16[1,5,96,768]{3,2,1,0:T(8,128)(2,1)}, u32[]{:S(2)}, u32[]{:S(2)}) collective-permute-start(bf16[1,5,96,768]{3,2,1,0:T(8,128)(2,1)} %bitcast.167), channel_id=1, source_target_pairs={{0,8},{4,12},{8,0},{12,4},{16,24},{20,28},{24,16},{28,20},{1,9},{5... | collective-permute-start | bytes 2211848 | tf_op jit(solution)/shard_map/ppermute | solution.py:68
  363.2 20.1 %collective-permute-start.33 = (bf16[1,5,96,768]{3,2,1,0:T(8,128)(2,1)}, bf16[1,5,96,768]{3,2,1,0:T(8,128)(2,1)S(1)}, u32[]{:S(2)}, u32[]{:S(2)}) collective-permute-start(bf16[1,5,96,768]{3,2,1,0:T(8,128)(2,1)} %bitcast.168), channel_id=1, source_target_pairs={{0,16},{4,20},{8,24},{12,28},{16,0},{20,4},{24,8},{28,12},{1,17},{... | collective-permute-start | bytes 2211848 | tf_op jit(solution)/shard_map/ppermute | solution.py:68
  364.7 17.9 %collective-permute-start.30 = (bf16[2,1,96,576]{2,3,1,0:T(8,128)(2,1)}, bf16[2,1,96,576]{2,3,1,0:T(8,128)(2,1)S(1)}, u32[]{:S(2)}, u32[]{:S(2)}) collective-permute-start(bf16[2,1,96,576]{2,3,1,0:T(8,128)(2,1)} %bitcast.144), channel_id=1, source_target_pairs={{0,8},{4,12},{8,0},{12,4},{16,24},{20,28},{24,16},{28,20},{1,9},{5... | collective-permute-start | bytes 663560 | tf_op jit(solution)/shard_map/ppermute | solution.py:68
  382.7 10.8 %collective-permute-start.31 = (bf16[1,96,576]{1,2,0:T(8,128)(2,1)S(1)}, bf16[1,96,576]{1,2,0:T(8,128)(2,1)S(1)}, u32[]{:S(2)}, u32[]{:S(2)}) collective-permute-start(bf16[1,96,576]{1,2,0:T(8,128)(2,1)S(1)} %slice_bitcast_fusion), channel_id=1, source_target_pairs={{0,16},{4,20},{8,24},{12,28},{16,0},{20,4},{24,8},{28,12},{1,17},{... | collective-permute-start | bytes 331784 | tf_op jit(solution)/shard_map/ppermute | solution.py:68
  (43 other events, 346.1 us)
Sparse Core Ops, SparseCore 0:
  15.2 36.8 all-gather.4
  59.8 35.8 all-gather.8
  97.3 35.9 all-gather.6
  220.4 32.3 reduce-scatter.5
  254.9 34.2 reduce-scatter.3
  302.3 34.7 reduce-scatter.7
